TPU v7x, 128 devices: a whole 4x4x4 slice. The times are simulated.
128 devices in a mesh: row: 8 (over x, core), col: 16 (over y, z).
Axes of the slice: x: 4, y: 4, z: 4, core: 2. Of those that a mesh axis runs over, the one named last changes fastest.
Arguments:
- latent: bfloat16 [16, 32, 32, 16], P(None, 'row', 'col'), may hold values from -6 to 6
- condition: bfloat16 [16, 1024], replicated, may hold values from -6 to 6
- caption: bfloat16 [16, 256, 4096], P('col'), may hold values from -6 to 6
- cap_len: int32 [16], replicated, may hold values from 8 to 256, as said below
- cotangent: bfloat16 [16, 32, 32, 16], P(None, 'row', 'col'), may hold values from -6 to 6
- embed_weight: bfloat16 [3, 3, 16, 1536], replicated, may hold values from -0.5 to 0.5
- modulate_weight: bfloat16 [1024, 6144], P(None, ('row', 'col')), may hold values from -0.1875 to 0.1875
- norm_gains: float32 [7, 1536], replicated, may hold values from 0.1 to 1.9
- cross_gate: float32 [24], replicated, may hold values from -1.5 to 1.5
- qkv_weight: bfloat16 [3, 1536, 1536], P(None, 'col', 'row'), may hold values from -0.15625 to 0.15625
- text_kv_weight: bfloat16 [2, 4096, 1536], P(None, 'col', 'row'), may hold values from -0.09375 to 0.09375
- out_weight: bfloat16 [1536, 1536], P('row', 'col'), may hold values from -0.15625 to 0.15625
- gate_up_weight: bfloat16 [2, 1536, 4096], P(None, 'col', 'row'), may hold values from -0.15625 to 0.15625
- down_weight: bfloat16 [4096, 1536], P('row', 'col'), may hold values from -0.09375 to 0.09375
- unpatch_weight: bfloat16 [3, 3, 1536, 16], replicated, may hold values from -0.0546875 to 0.0546875
Outputs:
- activation: bfloat16 [16, 32, 32, 16], P(None, 'row', 'col')
- latent_grad: bfloat16 [16, 32, 32, 16], P(None, 'row', 'col')
- embed_grad: float32 [3, 3, 16, 1536], replicated
- modulate_grad: float32 [1024, 6144], P(None, ('row', 'col'))
- gains_grad: float32 [7, 1536], replicated
- gate_grad: float32 [24], replicated
- qkv_grad: float32 [3, 1536, 1536], P(None, 'col', 'row')
- text_kv_grad: float32 [2, 4096, 1536], P(None, 'col', 'row')
- out_grad: float32 [1536, 1536], P('row', 'col')
- gate_up_grad: float32 [2, 1536, 4096], P(None, 'col', 'row')
- down_grad: float32 [4096, 1536], P('row', 'col')
- unpatch_grad: float32 [3, 3, 1536, 16], replicated
Inputs may be any that keep to these rules, and one draw needn't show every extreme that they name: `cap_len`: every image has 8 to 256 caption tokens; in every draw one image has exactly 256 and another exactly 8.
All inputs are finite; a program needn't handle non-finite values.
Results may differ from a plain program's by a relative error of at most 0.025.
Values may be sent and summed in bfloat16 or wider, within the bound.
No kernel may reach another device: no remote copies, remote signals or barrier semaphores. Data moves between devices by JAX's collectives and lax.ppermute only.
A program may use at most 256 MiB of HBM per device.

v0:
```python
import math
from functools import partial

import jax
import jax.numpy as jnp
import numpy as np
from jax import lax
from jax.experimental import pallas as pl
from jax.experimental.pallas import tpu as pltpu
from jax.sharding import PartitionSpec as P

HEADS = 24
HD = 64
GRID = 32
TOKENS = GRID * GRID
EPSILON = 1e-06
ROPE_BASE = 10000.0
MASKED = -1e30
F32 = jnp.float32
BF16 = jnp.bfloat16
ROWS = 8
COLS = 16
QUERY_BLOCK = 256
BLOCK = TOKENS // ROWS
PAIR = 2 * BLOCK
MIB = 2**20
SHARED = 320
CHUNK = 512
LIGHT = pl.CostEstimate(flops=1, bytes_accessed=1, transcendentals=0)


def dot(left, right, contract):
    return lax.dot_general(
        left, right, ((contract[:1], contract[1:]), ((), ())), preferred_element_type=F32
    )


def row_pairs(dx, dc):
    return [
        (((x + dx) % 4) * 2 + (c + dc) % 2, x * 2 + c) for x in range(4) for c in range(2)
    ]


def row_pairs_to(dx, dc):
    return [(dst, src) for src, dst in row_pairs(dx, dc)]


def from_chips(piece):
    return [piece] + [lax.ppermute(piece, "row", row_pairs(d, 0)) for d in (1, 2, 3)]


def with_other_core(pieces):
    quad = jnp.stack(pieces)
    return quad, lax.ppermute(quad, "row", row_pairs(0, 1))


def gather_near(piece):
    return with_other_core(from_chips(piece))


def sum_cores(own, other):
    other = lax.ppermute(other, "row", row_pairs(0, 1))
    return [(own[d].astype(F32) + other[d].astype(F32)).astype(BF16) for d in range(4)]


def to_chips(near):
    return [near[0]] + [lax.ppermute(near[d], "row", row_pairs_to(d, 0)) for d in (1, 2, 3)]


def col_pairs_to(dy, dz):
    return [(y * 4 + z, (y + dy) % 4 * 4 + (z + dz) % 4) for y in range(4) for z in range(4)]


def col_pairs(dy, dz):
    return [(dst, src) for src, dst in col_pairs_to(dy, dz)]


def from_col(piece, step):
    return [piece] + [lax.ppermute(piece, "col", col_pairs(*step(d))) for d in (1, 2, 3)]


def along_y(d):
    return (d, 0)


def along_z(d):
    return (0, d)


def along_col(parts, step):
    return [parts[0]] + [lax.ppermute(parts[d], "col", col_pairs_to(*step(d))) for d in (1, 2, 3)]


def send_all(piece, axis):
    copies = jnp.broadcast_to(piece, (lax.axis_size(axis),) + piece.shape)
    return lax.all_to_all(copies, axis, 0, 0)


def after(value, *others):
    return lax.optimization_barrier((value,) + others)[0]


def rope_tables():
    quarter = HD // 4
    frequency = np.float32(ROPE_BASE) ** (-np.arange(quarter, dtype=np.float32) / np.float32(quarter))
    place = np.arange(TOKENS)
    row = frequency[:, None] * (place // GRID).astype(np.float32)[None, :]
    col = frequency[:, None] * (place % GRID).astype(np.float32)[None, :]
    return np.stack([np.cos(row), np.sin(row), np.cos(col), np.sin(col)]).astype(np.float32)


def turn(v, table, sign):
    a, b, c, d = (v[k * 16 : (k + 1) * 16] for k in range(4))
    cr, sr, cc, sc = table[0], table[1] * sign, table[2], table[3] * sign
    return jnp.concatenate([a * cr - b * sr, a * sr + b * cr, c * cc - d * sc, c * sc + d * cc], 0)


def column_rms(v):
    return lax.rsqrt(jnp.mean(v * v, axis=0, keepdims=True) + EPSILON)


def normed(v, gain):
    return v * column_rms(v) * gain


def column_rms_back(v, u):
    scale = column_rms(v)
    return (u - v * (jnp.mean(u * v, axis=0, keepdims=True) * scale * scale)) * scale


def whole(shape):
    zeros = (0,) * len(shape)
    return pl.BlockSpec(shape, lambda *_: zeros, pipeline_mode=pl.Buffered(1))


def held():
    return pl.BlockSpec(memory_space=pltpu.VMEM)


def lane_block(rows, lanes):
    return pl.BlockSpec((rows, lanes), lambda t, *_: (0, t))


def row_block(rows, lanes):
    return pl.BlockSpec((rows, lanes), lambda t, *_: (t, 0))


def params(mib):
    return pltpu.CompilerParams(vmem_limit_bytes=mib * MIB, dimension_semantics=("arbitrary",))


def row_of_sums(v):
    return jnp.sum(v.T, axis=0, keepdims=True)


def attend_kernel(
    cap_ref, gate_ref, raw_ref, text_ref, gain_ref, table_ref, mixed_ref, lse_ref,
    q_ref, k_ref, v_ref, tk_ref, tv_ref,
):
    step = pl.program_id(0)
    heads = raw_ref.shape[1]

    @pl.when(step == 0)
    def _():
        table = table_ref[...]
        for h in range(heads):
            q = turn(normed(raw_ref[0, h], gain_ref[0, h]), table, 1.0).astype(BF16)
            q_ref[h] = q * jnp.asarray(0.125, BF16)
            k_ref[h] = turn(normed(raw_ref[1, h], gain_ref[1, h]), table, 1.0).T.astype(BF16)
            v_ref[h] = raw_ref[2, h].astype(BF16)
            tk_ref[h] = normed(text_ref[0, h], gain_ref[2, h]).T.astype(BF16)
            tv_ref[h] = text_ref[1, h].astype(BF16)

    slots = tk_ref.shape[1]
    mask = lax.broadcasted_iota(jnp.int32, (slots, QUERY_BLOCK), 0) < cap_ref[0]
    here = pl.ds(pl.multiple_of(step * QUERY_BLOCK, QUERY_BLOCK), QUERY_BLOCK)
    outs = []
    for h in range(heads):
        qb = q_ref[h, :, here]
        e = jnp.exp(dot(k_ref[h], qb, (1, 0)))
        total = jnp.sum(e, axis=0, keepdims=True)
        own = dot(v_ref[h], e.astype(BF16), (1, 0)) / total
        te = jnp.exp(jnp.where(mask, dot(tk_ref[h], qb, (1, 0)), MASKED))
        text_total = jnp.sum(te, axis=0, keepdims=True)
        text = dot(tv_ref[h], te.astype(BF16), (1, 0)) / text_total
        outs.append(own + gate_ref[h] * text)
        lse_ref[h, 0:1] = jnp.log(total)
        lse_ref[h, 1:2] = jnp.log(text_total)
    mixed_ref[...] = jnp.concatenate(outs, 0).astype(BF16)


def attend(raw, text_raw, gains, table, cap, gates):
    heads = raw.shape[1]
    slots = text_raw.shape[3]
    return pl.pallas_call(
        attend_kernel,
        grid_spec=pltpu.PrefetchScalarGridSpec(
            num_scalar_prefetch=2,
            grid=(TOKENS // QUERY_BLOCK,),
            in_specs=[
                whole((3, heads, HD, TOKENS)),
                whole((2, heads, HD, slots)),
                whole((3, heads, HD, 1)),
                whole((4, 16, TOKENS)),
            ],
            out_specs=[
                lane_block(heads * HD, QUERY_BLOCK),
                pl.BlockSpec((heads, 8, QUERY_BLOCK), lambda t, *_: (0, 0, t)),
            ],
            scratch_shapes=[
                pltpu.VMEM((heads, HD, TOKENS), BF16),
                pltpu.VMEM((heads, TOKENS, HD), BF16),
                pltpu.VMEM((heads, HD, TOKENS), BF16),
                pltpu.VMEM((heads, slots, HD), BF16),
                pltpu.VMEM((heads, HD, slots), BF16),
            ],
        ),
        out_shape=[
            jax.ShapeDtypeStruct((heads * HD, TOKENS), BF16),
            jax.ShapeDtypeStruct((heads, 8, TOKENS), F32),
        ],
        compiler_params=params(20),
        cost_estimate=LIGHT,
        name="attend",
    )(cap, gates, raw, text_raw, gains, table)


def text_back_kernel(
    cap_ref, gate_ref, q_raw_ref, text_ref, gain_ref, table_ref, lse_ref, grad_ref, caption_ref, held_ref,
    grads_ref, dq_ref, d_gain_ref, low_ref,
):
    del held_ref
    step = pl.program_id(0)
    heads, _, slots = low_ref.shape[1:]

    @pl.when(step == 0)
    def _():
        table = table_ref[...]
        mask = lax.broadcasted_iota(jnp.int32, (slots, TOKENS), 0) < cap_ref[0]
        for h in range(heads):
            gate = gate_ref[h]
            q = turn(normed(q_raw_ref[h], gain_ref[0, h]), table, 1.0).astype(BF16)
            q = q * jnp.asarray(0.125, BF16)
            tk = normed(text_ref[0, h], gain_ref[2, h]).astype(BF16)
            tv = text_ref[1, h].astype(BF16)
            g = grad_ref[h]
            tp = jnp.exp(jnp.where(mask, dot(tk, q, (0, 0)), MASKED) - lse_ref[h, 1:2])
            tpb = tp.astype(BF16)
            low_ref[1, h] = (dot(g, tpb, (1, 1)) * gate).astype(BF16)
            gate_terms = g.astype(F32) * dot(tv, tpb, (1, 0))
            tpd = tp * dot(tv, g, (0, 0)) * gate
            dts = (tpd - tp * jnp.sum(tpd, axis=0, keepdims=True)).astype(BF16)
            dq_ref[h] = dot(tk, dts, (1, 0))
            d_tk = dot(q, dts, (1, 1))
            values = text_ref[0, h]
            low_ref[0, h] = column_rms_back(values, d_tk * gain_ref[2, h]).astype(BF16)
            d_gain_ref[h, 0:1] = row_of_sums(values * column_rms(values) * d_tk)
            d_gain_ref[h, 1:2] = row_of_sums(gate_terms)

    d_text = low_ref[...].reshape(2 * heads * HD, slots)
    rows = grads_ref.shape[1]
    for k in range(grads_ref.shape[0]):
        grads_ref[k] = dot(caption_ref[:, k * rows : (k + 1) * rows], d_text, (0, 1)).astype(BF16)


def text_back(raw, text_raw, gains, table, lse, grads, cap, gates, caption, held):
    heads = raw.shape[1]
    slots = text_raw.shape[3]
    rows = caption.shape[1] // COLS
    lanes = 2 * heads * HD
    return pl.pallas_call(
        text_back_kernel,
        grid_spec=pltpu.PrefetchScalarGridSpec(
            num_scalar_prefetch=2,
            grid=(4,),
            in_specs=[
                pl.BlockSpec((None, heads, HD, TOKENS), lambda t, *_: (0, 0, 0, 0)),
                whole(text_raw.shape),
                whole(gains.shape),
                whole(table.shape),
                whole(lse.shape),
                whole(grads.shape),
                pl.BlockSpec((slots, 4 * rows), lambda t, *_: (0, t)),
                pl.BlockSpec(memory_space=pl.ANY),
            ],
            out_specs=[
                pl.BlockSpec((4, rows, lanes), lambda t, *_: (t, 0, 0)),
                pl.BlockSpec((heads, HD, TOKENS), lambda t, *_: (0, 0, 0)),
                pl.BlockSpec((heads, 8, HD), lambda t, *_: (0, 0, 0)),
            ],
            scratch_shapes=[pltpu.VMEM((2, heads, HD, slots), BF16)],
        ),
        out_shape=[
            jax.ShapeDtypeStruct(held.shape, BF16),
            jax.ShapeDtypeStruct((heads, HD, TOKENS), F32),
            jax.ShapeDtypeStruct((heads, 8, HD), F32),
        ],
        input_output_aliases={9: 0},
        compiler_params=params(58),
        cost_estimate=LIGHT,
        name="text_back",
    )(cap, gates, raw, text_raw, gains, table, lse, grads, caption, held)


def attend_back_kernel(
    raw_ref, gain_ref, table_ref, lse_ref, grad_ref, dq_text_ref,
    d_raw_ref, d_gain_ref, dv_ref, dk_ref, dq_ref,
):
    table = table_ref[...]
    q = turn(normed(raw_ref[0], gain_ref[0]), table, 1.0).astype(BF16) * jnp.asarray(0.125, BF16)
    k = turn(normed(raw_ref[1], gain_ref[1]), table, 1.0)
    k, k_turned = k.astype(BF16), k.T.astype(BF16)
    v_turned = raw_ref[2].T.astype(BF16)
    for first in range(0, TOKENS, QUERY_BLOCK):
        here = slice(first, first + QUERY_BLOCK)
        qb = q[:, here]
        gb = grad_ref[:, here]
        p = jnp.exp(dot(k_turned, qb, (1, 0)) - lse_ref[0:1, here])
        dv = dot(gb, p.astype(BF16), (1, 1))
        pd = p * dot(v_turned, gb, (1, 0))
        ds = (pd - p * jnp.sum(pd, axis=0, keepdims=True)).astype(BF16)
        dq_ref[:, here] = dot(k, ds, (1, 0)) + dq_text_ref[:, here]
        dk = dot(qb, ds, (1, 1))
        if first == 0:
            dv_ref[...] = dv
            dk_ref[...] = dk
        else:
            dv_ref[...] += dv
            dk_ref[...] += dk

    def raw_back(which, d_turned):
        spun = turn(d_turned.astype(BF16).astype(F32), table, -1.0)
        values = raw_ref[which]
        d_raw_ref[which] = column_rms_back(values, spun * gain_ref[which]).astype(BF16)
        d_gain_ref[which : which + 1] = row_of_sums(values * column_rms(values) * spun)

    raw_back(0, dq_ref[...] * 0.125)
    raw_back(1, dk_ref[...])
    d_raw_ref[2] = dv_ref[...].astype(BF16)


def attend_back(raw, gains, table, lse, grads, dq_text):
    heads = raw.shape[1]
    return pl.pallas_call(
        attend_back_kernel,
        grid=(heads,),
        in_specs=[
            pl.BlockSpec((3, None, HD, TOKENS), lambda h: (0, h, 0, 0)),
            pl.BlockSpec((3, None, HD, 1), lambda h: (0, h, 0, 0)),
            pl.BlockSpec((4, 16, TOKENS), lambda h: (0, 0, 0)),
            pl.BlockSpec((None, 8, TOKENS), lambda h: (h, 0, 0)),
            pl.BlockSpec((None, HD, TOKENS), lambda h: (h, 0, 0)),
            pl.BlockSpec((None, HD, TOKENS), lambda h: (h, 0, 0)),
        ],
        out_specs=[
            pl.BlockSpec((3, None, HD, TOKENS), lambda h: (0, h, 0, 0)),
            pl.BlockSpec((None, 8, HD), lambda h: (h, 0, 0)),
        ],
        scratch_shapes=[pltpu.VMEM((HD, TOKENS), F32) for _ in range(3)],
        out_shape=[
            jax.ShapeDtypeStruct((3, heads, HD, TOKENS), BF16),
            jax.ShapeDtypeStruct((heads, 8, HD), F32),
        ],
        compiler_params=params(58),
        cost_estimate=LIGHT,
        name="attend_back",
    )(raw, gains, table, lse, grads, dq_text)


def tile_places(chunk_first):
    r, c, k = np.meshgrid(np.arange(ROWS), np.arange(COLS), np.arange(8), indexing="ij")
    token = r * BLOCK + (k // 2) * GRID + c * 2 + k % 2
    source = (k * ROWS + r) * COLS + c if chunk_first else (r * COLS + c) * 8 + k
    places = np.zeros((TOKENS, TOKENS), np.float32)
    places[source.ravel(), token.ravel()] = 1.0
    return jnp.asarray(places, BF16)


def grid_shift(field, di, dj):
    step = di * GRID + dj
    moved = pltpu.roll(field, (-step) % TOKENS, 1) if step else field
    place = lax.broadcasted_iota(jnp.int32, field.shape, 1)
    row = place // GRID + di
    col = place % GRID + dj
    inside = (row >= 0) & (row < GRID) & (col >= 0) & (col < GRID)
    return jnp.where(inside, moved, 0.0)


def image_kernel(packed_ref, place_ref, patch_ref, cot_ref):
    for which, sign, out_ref in ((0, 1, patch_ref), (1, -1, cot_ref)):
        lanes = slice(which * 128, (which + 1) * 128)
        tiles = jnp.concatenate([packed_ref[r, :, lanes] for r in range(ROWS)], 0)
        turned = tiles.astype(F32).T
        chunks = jnp.concatenate([turned[k * 16 : (k + 1) * 16] for k in range(8)], 1)
        image = dot(chunks.astype(BF16), place_ref[...], (1, 0))
        for a in range(3):
            for b in range(3):
                first = (a * 3 + b) * 16
                out_ref[first : first + 16] = grid_shift(
                    image, sign * (a - 1), sign * (b - 1)
                ).astype(BF16)


def image_taps(packed):
    out = jax.ShapeDtypeStruct((144, TOKENS), BF16)
    return pl.pallas_call(
        image_kernel,
        out_shape=[out, out],
        compiler_params=pltpu.CompilerParams(vmem_limit_bytes=12 * MIB),
        cost_estimate=LIGHT,
        name="image_taps",
    )(packed, tile_places(True))


def field_of(taps, place, sign):
    total = jnp.zeros((16, TOKENS), F32)
    for a in range(3):
        for b in range(3):
            first = (a * 3 + b) * 16
            total = total + grid_shift(taps[first : first + 16], sign * (a - 1), sign * (b - 1))
    tiles = dot(total.astype(BF16), place, (1, 1))
    return [tiles[:, r * BLOCK : (r + 1) * BLOCK] for r in range(ROWS)]


def row_rms(v):
    return lax.rsqrt(jnp.mean(v * v, axis=-1, keepdims=True) + EPSILON)


def row_rms_back(v, scale, u):
    return (u - v * (jnp.mean(u * v, axis=-1, keepdims=True) * scale * scale)) * scale


def unpack_kernel(at_ref, *refs):
    piece_refs, (joined_ref, out_ref, turn_ref) = refs[:4], refs[4:]
    part = piece_refs[0].shape[1] // 2
    local_width = piece_refs[0].shape[2] // 2
    for dz in range(4):
        for dy in range(4):
            c = lax.rem(at_ref[2] + dy, 4) * 4 + lax.rem(at_ref[3] + dz, 4)
            rows = pl.ds(pl.multiple_of(c * part, part), part)
            piece = piece_refs[dz][dy]
            joined_ref[0, rows, :] = piece[:part, :local_width]
            joined_ref[1, rows, :] = piece[:part, local_width:]
            joined_ref[2, rows, :] = piece[part:, :local_width]
            turn_ref[rows, :] = piece[part:, local_width:]
    out_ref[...] = turn_ref[...].T


def unpack_head(at, pieces):
    _, rows, lanes = pieces[0].shape
    width, local_width = COLS * rows // 2, lanes // 2
    return pl.pallas_call(
        unpack_kernel,
        grid_spec=pltpu.PrefetchScalarGridSpec(
            num_scalar_prefetch=1,
            grid=(1,),
            in_specs=[whole(pieces[0].shape)] * 4,
            out_specs=[
                pl.BlockSpec((3, width, local_width), lambda t, at: (0, 0, 0)),
                pl.BlockSpec((local_width, width), lambda t, at: (0, 0)),
            ],
            scratch_shapes=[pltpu.VMEM((width, local_width), BF16)],
        ),
        out_shape=[
            jax.ShapeDtypeStruct((3, width, local_width), BF16),
            jax.ShapeDtypeStruct((local_width, width), BF16),
        ],
        compiler_params=params(14),
        cost_estimate=LIGHT,
        name="unpack_head",
    )(at, *pieces)


def text_kernel(at_ref, p0_ref, p1_ref, p2_ref, p3_ref, caption_ref, raw_ref):
    rows = p0_ref.shape[1]
    total = 0.0
    for dy, ref in enumerate((p0_ref, p1_ref, p2_ref, p3_ref)):
        for dz in range(4):
            c = lax.rem(at_ref[2] + dy, 4) * 4 + lax.rem(at_ref[3] + dz, 4)
            lanes = pl.ds(pl.multiple_of(c * rows, rows), rows)
            total = total + dot(ref[dz], caption_ref[:, lanes], (0, 1))
    raw_ref[...] = total


def text_project(at, pieces, caption):
    lanes = pieces[0].shape[2]
    slots = caption.shape[0]
    return pl.pallas_call(
        text_kernel,
        grid_spec=pltpu.PrefetchScalarGridSpec(
            num_scalar_prefetch=1,
            grid=(1,),
            in_specs=[whole(pieces[0].shape)] * 4 + [whole(caption.shape)],
            out_specs=pl.BlockSpec((lanes, slots), lambda t, at: (0, 0)),
        ),
        out_shape=jax.ShapeDtypeStruct((lanes, slots), F32),
        compiler_params=params(16),
        cost_estimate=LIGHT,
        name="text_project",
    )(at, *pieces, caption)


def qkv_kernel(patch_ref, embed_ref, vec_ref, weight_ref, raw_ref):
    x = dot(patch_ref[...], embed_ref[...], (0, 0))
    h = (x * row_rms(x) * vec_ref[0:1]).astype(BF16)
    for s in range(3):
        raw_ref[s] = dot(h, weight_ref[s], (1, 0)).T


def qkv_project(patches, embed, vec, weight):
    part = weight.shape[2]
    return pl.pallas_call(
        qkv_kernel,
        grid=(TOKENS // PAIR,),
        in_specs=[lane_block(144, PAIR), whole(embed.shape), whole(vec.shape), whole(weight.shape)],
        out_specs=pl.BlockSpec((3, part, PAIR), lambda t: (0, 0, t)),
        out_shape=jax.ShapeDtypeStruct((3, part, TOKENS), F32),
        compiler_params=params(16),
        cost_estimate=LIGHT,
        name="qkv_project",
    )(patches, embed, vec, weight)


def joined(ref):
    return ref[...].reshape(-1, ref.shape[2])


def halves(core, first, second):
    return jnp.where(core == 0, first, second)


def forward_kernel(
    at_ref, near_ref, far_ref, out_near_ref, out_far_ref, patch_ref, embed_ref, vec_ref, ffn_ref,
    attn_ref, second_ref, gate_up_ref, hidden_ref, own_ref, other_ref,
):
    core = at_ref[1]
    hidden_width = hidden_ref.shape[1]
    x = dot(patch_ref[...], embed_ref[...], (0, 0))
    attn = dot(joined(near_ref), joined(out_near_ref), (0, 0))
    attn = attn + dot(joined(far_ref), joined(out_far_ref), (0, 0))
    attn_ref[...] = attn.astype(BF16)
    mid = x + vec_ref[1:2] * (attn * row_rms(attn))
    second = (mid * row_rms(mid) * vec_ref[2:3]).astype(BF16)
    second_ref[...] = second
    gate_up = dot(second, ffn_ref[:, : 2 * hidden_width], (1, 0))
    gate_up_ref[...] = gate_up.astype(BF16)
    gate = gate_up[:, :hidden_width]
    hidden = (gate * jax.nn.sigmoid(gate) * gate_up[:, hidden_width:]).astype(BF16)
    hidden_ref[...] = hidden
    part = dot(hidden, ffn_ref[:, 2 * hidden_width :], (1, 1)).astype(BF16)
    own_ref[0] = halves(core, part[:BLOCK], part[BLOCK:])
    other_ref[0] = halves(core, part[BLOCK:], part[:BLOCK])


def forward(at, mixed, out_whole, patches, embed, vec, ffn):
    width = embed.shape[1]
    part = mixed[0].shape[1]
    hidden_width = ffn.shape[1] // 3
    by_chip = pl.BlockSpec((1, BLOCK, width), lambda t, at: ((t - at[0] + 4) % 4, 0, 0))
    return pl.pallas_call(
        forward_kernel,
        grid_spec=pltpu.PrefetchScalarGridSpec(
            num_scalar_prefetch=1,
            grid=(4,),
            in_specs=[
                pl.BlockSpec((4, part, PAIR), lambda t, at: (0, 0, t)),
                pl.BlockSpec((4, part, PAIR), lambda t, at: (0, 0, t)),
                whole((4, part, width)),
                whole((4, part, width)),
                lane_block(144, PAIR),
                whole(embed.shape),
                whole(vec.shape),
                whole(ffn.shape),
            ],
            out_specs=[
                row_block(PAIR, width),
                row_block(PAIR, width),
                row_block(PAIR, 2 * hidden_width),
                row_block(PAIR, hidden_width),
                by_chip,
                by_chip,
            ],
        ),
        out_shape=[
            jax.ShapeDtypeStruct((TOKENS, width), BF16),
            jax.ShapeDtypeStruct((TOKENS, width), BF16),
            jax.ShapeDtypeStruct((TOKENS, 2 * hidden_width), BF16),
            jax.ShapeDtypeStruct((TOKENS, hidden_width), BF16),
            jax.ShapeDtypeStruct((4, BLOCK, width), BF16),
            jax.ShapeDtypeStruct((4, BLOCK, width), BF16),
        ],
        compiler_params=params(56),
        cost_estimate=LIGHT,
        name="forward",
    )(at, *mixed, *out_whole, patches, embed, vec, ffn)


def own_grad_kernel(p0_ref, p1_ref, p2_ref, p3_ref, cot_ref, unpatch_ref, vec_ref, d_ffn_ref, ffn_ref):
    ffn = sum(p[...].astype(F32) for p in (p0_ref, p1_ref, p2_ref, p3_ref))
    ffn_ref[...] = ffn
    d_last = dot(cot_ref[...], unpatch_ref[...], (0, 0))
    d_ffn_ref[...] = row_rms_back(ffn, row_rms(ffn), vec_ref[3:4] * d_last).astype(BF16)


def own_grad(pieces, cot_own, unpatch, vec):
    shape = (BLOCK, unpatch.shape[1])
    return pl.pallas_call(
        own_grad_kernel,
        out_shape=[jax.ShapeDtypeStruct(shape, BF16), jax.ShapeDtypeStruct(shape, F32)],
        compiler_params=pltpu.CompilerParams(vmem_limit_bytes=58 * MIB),
        cost_estimate=LIGHT,
        name="own_grad",
    )(*pieces, cot_own, unpatch, vec)


def own_kernel(
    at_ref, ffn_ref, attn_ref, patch_ref, cot_ref, embed_ref, unpatch_ref, vec_ref, place_ref,
    field_ref, unpatch_sum_ref, sums_ref, taps_ref,
):
    ffn = ffn_ref[...]
    d_last = dot(cot_ref[...], unpatch_ref[...], (0, 0))
    normed_ffn = ffn * row_rms(ffn)
    sums_ref[...] = jnp.broadcast_to(
        jnp.sum(normed_ffn * d_last, axis=0, keepdims=True), sums_ref.shape
    )
    attn = attn_ref[...].astype(F32)
    x = dot(patch_ref[...], embed_ref[...], (0, 0))
    last = (x + vec_ref[1:2] * (attn * row_rms(attn)) + vec_ref[3:4] * normed_ffn).astype(BF16)
    unpatch_sum_ref[...] = dot(cot_ref[...], last, (1, 0))
    taps_ref[...] = jnp.zeros_like(taps_ref)
    here = pl.multiple_of((2 * at_ref[0] + at_ref[1]) * BLOCK, BLOCK)
    taps_ref[:, pl.ds(here, BLOCK)] = dot(unpatch_ref[...], last, (1, 1))
    for r, tile in enumerate(field_of(taps_ref[...], place_ref[...], 1)):
        field_ref[r] = tile


def own_block(at, ffn, attn, patches, cot_taps, embed, unpatch, vec, place):
    width = embed.shape[1]
    lanes = pl.BlockSpec((144, BLOCK), lambda t, at: (0, 2 * at[0] + at[1]))
    return pl.pallas_call(
        own_kernel,
        grid_spec=pltpu.PrefetchScalarGridSpec(
            num_scalar_prefetch=1,
            grid=(1,),
            in_specs=[
                whole((BLOCK, width)),
                pl.BlockSpec((BLOCK, width), lambda t, at: (2 * at[0] + at[1], 0)),
                lanes,
                lanes,
                whole(embed.shape),
                whole(unpatch.shape),
                whole(vec.shape),
                whole(place.shape),
            ],
            out_specs=[
                pl.BlockSpec((ROWS, 16, BLOCK), lambda t, at: (0, 0, 0)),
                pl.BlockSpec((144, width), lambda t, at: (0, 0)),
                pl.BlockSpec((8, width), lambda t, at: (0, 0)),
            ],
            scratch_shapes=[pltpu.VMEM((144, TOKENS), F32)],
        ),
        out_shape=[
            jax.ShapeDtypeStruct((ROWS, 16, BLOCK), F32),
            jax.ShapeDtypeStruct((144, width), F32),
            jax.ShapeDtypeStruct((8, width), F32),
        ],
        compiler_params=params(14),
        cost_estimate=LIGHT,
        name="own_block",
    )(at, ffn, attn, patches, cot_taps, embed, unpatch, vec, place)


def backward_kernel(
    at_ref, own_ref, other_ref, ffn_ref, out_near_ref, out_far_ref, gate_up_ref, attn_ref,
    patch_ref, embed_ref, cot_ref, unpatch_ref, vec_ref,
    d_ffn_ref, d_gate_up_ref, d_attn_ref, d_mid_ref, mixed_own_ref, mixed_other_ref, sums_ref,
):
    step = pl.program_id(0)
    chip, core = at_ref[0], at_ref[1]
    hidden_width = d_gate_up_ref.shape[1] // 2
    own, other = own_ref[0], other_ref[0]
    d_ffn = jnp.concatenate([halves(core, own, other), halves(core, other, own)], 0)
    d_ffn_ref[...] = d_ffn
    d_hidden = dot(d_ffn, ffn_ref[:, 2 * hidden_width :], (1, 0))
    gate = gate_up_ref[:, :hidden_width].astype(F32)
    up = gate_up_ref[:, hidden_width:].astype(F32)
    sigma = jax.nn.sigmoid(gate)
    silu = gate * sigma
    d_gate = d_hidden * up * (sigma + silu * (1.0 - sigma))
    d_gate_up = jnp.concatenate([d_gate.astype(BF16), (d_hidden * silu).astype(BF16)], 1)
    d_gate_up_ref[...] = d_gate_up
    d_second = dot(d_gate_up, ffn_ref[:, : 2 * hidden_width], (1, 1))

    x = dot(patch_ref[...], embed_ref[...], (0, 0))
    attn = attn_ref[...].astype(F32)
    attn_scale = row_rms(attn)
    attn_normed = attn * attn_scale
    mid = x + vec_ref[1:2] * attn_normed
    mid_scale = row_rms(mid)
    mid_sum = jnp.sum(mid * mid_scale * d_second, axis=0, keepdims=True)
    d_last = dot(cot_ref[...], unpatch_ref[...], (0, 0))
    place = lax.broadcasted_iota(jnp.int32, (PAIR, 1), 0) // BLOCK
    mine = (place == core) & (step == chip)
    d_mid = row_rms_back(mid, mid_scale, vec_ref[2:3] * d_second) + jnp.where(mine, d_last, 0.0)
    d_mid_ref[...] = d_mid.astype(BF16)
    attn_sum = jnp.sum(attn_normed * d_mid, axis=0, keepdims=True)
    d_attn = row_rms_back(attn, attn_scale, vec_ref[1:2] * d_mid).astype(BF16)
    d_attn_ref[...] = d_attn
    for weight_ref, part_ref in ((out_near_ref, mixed_own_ref), (out_far_ref, mixed_other_ref)):
        part_ref[...] = dot(joined(weight_ref), d_attn, (1, 1)).astype(BF16).reshape(part_ref.shape)

    @pl.when(step == 0)
    def _():
        sums_ref[...] = jnp.zeros_like(sums_ref)

    sums_ref[0:1] += mid_sum
    sums_ref[1:2] += attn_sum


def backward(at, d_ffn, ffn, out_whole, gate_up, attn, patches, embed, cot_taps, unpatch, vec):
    width = embed.shape[1]
    part = out_whole[0].shape[1]
    hidden_width = ffn.shape[1] // 3
    by_chip = pl.BlockSpec((1, BLOCK, width), lambda t, at: ((t - at[0] + 4) % 4, 0, 0))
    parts = pl.BlockSpec((4, part, PAIR), lambda t, at: (0, 0, t))
    return pl.pallas_call(
        backward_kernel,
        grid_spec=pltpu.PrefetchScalarGridSpec(
            num_scalar_prefetch=1,
            grid=(4,),
            in_specs=[
                by_chip,
                by_chip,
                held(),
                held(),
                held(),
                row_block(PAIR, 2 * hidden_width),
                row_block(PAIR, width),
                lane_block(144, PAIR),
                whole(embed.shape),
                lane_block(144, PAIR),
                whole(unpatch.shape),
                whole(vec.shape),
            ],
            out_specs=[
                row_block(PAIR, width),
                row_block(PAIR, 2 * hidden_width),
                row_block(PAIR, width),
                row_block(PAIR, width),
                parts,
                parts,
                pl.BlockSpec((8, width), lambda t, at: (0, 0)),
            ],
        ),
        out_shape=[
            jax.ShapeDtypeStruct((TOKENS, width), BF16),
            jax.ShapeDtypeStruct((TOKENS, 2 * hidden_width), BF16),
            jax.ShapeDtypeStruct((TOKENS, width), BF16),
            jax.ShapeDtypeStruct((TOKENS, width), BF16),
            jax.ShapeDtypeStruct((4, part, TOKENS), BF16),
            jax.ShapeDtypeStruct((4, part, TOKENS), BF16),
            jax.ShapeDtypeStruct((8, width), F32),
        ],
        compiler_params=params(32),
        cost_estimate=LIGHT,
        name="backward",
    )(at, *d_ffn, ffn, *out_whole, gate_up, attn, patches, embed, cot_taps, unpatch, vec)


def weight_kernel(
    second_ref, d_gate_up_ref, d_ffn_ref, hidden_ref, near_ref, far_ref, d_attn_ref,
    grads_ref, out_near_ref, out_far_ref,
):
    step = pl.program_id(0)
    chunk, _, lanes = grads_ref.shape[0] // 4, *grads_ref.shape[1:]
    part = second_ref.shape[1] // chunk
    rows = jnp.concatenate(
        [
            dot(second_ref[...], d_gate_up_ref[...], (0, 0)).astype(BF16),
            dot(d_ffn_ref[...], hidden_ref[...], (0, 0)).astype(BF16),
        ],
        1,
    )
    groups = rows.shape[1] // lanes
    first = grads_ref.shape[1] - groups * part
    for c in range(chunk):
        for g in range(groups):
            grads_ref[step * chunk + c, first + g * part : first + (g + 1) * part] = rows[
                c * part : (c + 1) * part, g * lanes : (g + 1) * lanes
            ]
    out_near_ref[0] = dot(near_ref[0], d_attn_ref[...], (1, 0)).astype(BF16)
    out_far_ref[0] = dot(far_ref[0], d_attn_ref[...], (1, 0)).astype(BF16)


def weight_grads(second, d_gate_up, d_ffn, hidden, mixed, d_attn, text_rows):
    width = second.shape[1]
    heads_width = mixed[0].shape[1]
    lanes = 2 * heads_width
    grads = (COLS, text_rows + width // COLS * 3 * hidden.shape[1] // lanes, lanes)
    pieces = pl.BlockSpec((1, heads_width, TOKENS), lambda t: (t, 0, 0))
    out_piece = pl.BlockSpec((1, heads_width, width), lambda t: (t, 0, 0))
    out_shape = jax.ShapeDtypeStruct((4, heads_width, width), BF16)
    return pl.pallas_call(
        weight_kernel,
        grid=(4,),
        in_specs=[
            lane_block(TOKENS, width // 4),
            whole(d_gate_up.shape),
            lane_block(TOKENS, width // 4),
            whole(hidden.shape),
            pieces,
            pieces,
            whole(d_attn.shape),
        ],
        out_specs=[pl.BlockSpec(grads, lambda t: (0, 0, 0)), out_piece, out_piece],
        out_shape=[jax.ShapeDtypeStruct(grads, BF16), out_shape, out_shape],
        compiler_params=params(40),
        cost_estimate=LIGHT,
        name="weight_grads",
    )(second, d_gate_up, d_ffn, hidden, *mixed, d_attn)


def first_kernel(
    at_ref, gate_ref, patch_ref, embed_ref, vec_ref, weight_ref, d_raw_ref, d_mid_ref, place_ref, out_sum_ref,
    unpatch_sum_ref, back_sums_ref, own_sums_ref, head_ref, text_head_ref, gains_ref, mod_ref, activation_ref,
    own_pack_ref, other_pack_ref, p0_ref, p1_ref, p2_ref, p3_ref,
    taps_acc, embed_acc, first_acc, shared_acc, qkv_acc, turned_acc,
):
    step = pl.program_id(0)
    last = pl.num_programs(0) - 1
    x = dot(patch_ref[...], embed_ref[...], (0, 0))
    scale = row_rms(x)
    x_normed = x * scale
    h = (x_normed * vec_ref[0:1]).astype(BF16)
    d_h = dot(d_raw_ref[0], weight_ref[0], (0, 1))
    for s in (1, 2):
        d_h = d_h + dot(d_raw_ref[s], weight_ref[s], (0, 1))

    @pl.when(step == 0)
    def _():
        qkv_acc[...] = jnp.zeros_like(qkv_acc)
        embed_acc[...] = jnp.zeros_like(embed_acc)
        first_acc[...] = jnp.zeros_like(first_acc)

    qkv_acc[...] += dot(joined(d_raw_ref), h, (1, 0)).reshape(qkv_acc.shape)
    first_acc[0:1] += jnp.sum(x_normed * d_h, axis=0, keepdims=True)
    d_first = (d_mid_ref[...].astype(F32) + row_rms_back(x, scale, vec_ref[0:1] * d_h)).astype(BF16)
    embed_acc[...] += dot(patch_ref[...], d_first, (1, 0))
    here = pl.ds(pl.multiple_of(step * PAIR, PAIR), PAIR)
    taps_acc[:, here] = dot(embed_ref[...], d_first, (1, 1))

    @pl.when(step == last)
    def _():
        part = p0_ref.shape[1] // 2
        for s in range(4):
            turned_acc[s] = (qkv_acc[s] if s < 3 else out_sum_ref[...]).T.astype(BF16)
        for dz, ref in enumerate((p0_ref, p1_ref, p2_ref, p3_ref)):
            z = lax.rem(at_ref[3] + dz, 4)
            for y in range(4):
                dy = lax.rem(y - at_ref[2] + 4, 4)
                first = pl.multiple_of((y * 4 + z) * part, part)
                pieces = [turned_acc[s, pl.ds(first, part), :] for s in range(4)]
                for k in range(2):
                    ref[dy, k * part : (k + 1) * part] = jnp.concatenate(
                        pieces[2 * k : 2 * k + 2], 1
                    )
        terms = jnp.concatenate(
            [first_acc[0:1], back_sums_ref[1:2], back_sums_ref[0:1], own_sums_ref[0:1]], 0
        )
        gates = [jnp.tanh(mod_ref[k : k + 1]) for k in (1, 3)]
        into = jnp.concatenate(
            [1.0 + mod_ref[0:1], gates[0], 1.0 + mod_ref[2:3], gates[1]], 0
        )
        d_gains = terms * into
        slope = jnp.concatenate(
            [jnp.ones_like(gates[0]), 1.0 - gates[0] * gates[0]] * 1
            + [jnp.ones_like(gates[0]), 1.0 - gates[1] * gates[1]],
            0,
        )
        d_modulation = terms * gains_ref[0:4] * slope
        heads = head_ref.shape[0]
        width = d_gains.shape[1]
        rows = [head_ref[h] for h in range(heads)], [text_head_ref[h] for h in range(heads)]
        own = jnp.concatenate(
            [
                jnp.concatenate([r[0:2] for r in rows[0]], 1),
                jnp.concatenate([r[0:1] for r in rows[1]], 1),
                jnp.zeros((5, heads * HD), F32),
            ],
            0,
        )
        own = jnp.concatenate([own, jnp.zeros((8, width - heads * HD), F32)], 1)
        row_at = 2 * at_ref[0] + at_ref[1]
        own = pltpu.roll(own, row_at * (heads * HD), 1)
        lane = lax.broadcasted_iota(jnp.int32, (1, width), 1)
        gate_row = jnp.zeros((1, width), F32)
        for h in range(heads):
            total = jnp.sum(rows[1][h][1:2], axis=1, keepdims=True)
            total = total * (1.0 - gate_ref[h] * gate_ref[h])
            gate_row = gate_row + jnp.where(lane == row_at * heads + h, total, 0.0)
        small = jnp.concatenate(
            [d_gains, own[0:3], gate_row, jnp.zeros((24, width), F32)], 0
        )
        for tile in range(12):
            lanes = slice(tile * 128, (tile + 1) * 128)
            first = tile * SHARED
            shared_acc[first : first + 144] = embed_acc[:, lanes].astype(BF16)
            shared_acc[first + 144 : first + 288] = unpatch_sum_ref[:, lanes].astype(BF16)
            shared_acc[first + 288 : first + SHARED] = small[:, lanes].astype(BF16)
        shared_acc[12 * SHARED :] = jnp.zeros((8 * CHUNK - 12 * SHARED, 128), BF16)
        latent = field_of(taps_acc[...], place_ref[...], -1)
        rows = [
            d_modulation[q : q + 1, tile * 128 : (tile + 1) * 128]
            for q in range(4)
            for tile in range(12)
        ]
        for r in range(ROWS):
            ahead = lax.rem(r // 2 - at_ref[0] + 4, 4)
            mods = jnp.concatenate(rows[6 * r : 6 * r + 6] + [jnp.zeros((10, 128), F32)], 0)
            piece = jnp.concatenate(
                [
                    shared_acc[r * CHUNK : (r + 1) * CHUNK],
                    activation_ref[r].astype(BF16),
                    latent[r].astype(BF16),
                    mods.astype(BF16),
                ],
                0,
            )

            @pl.when(at_ref[1] == r % 2)
            def _():
                own_pack_ref[ahead] = piece

            @pl.when(at_ref[1] != r % 2)
            def _():
                other_pack_ref[ahead] = piece


def first_back(
    at, gates, patches, embed, vec, weight, d_raw, d_mid, place, out_sum, unpatch_sum, back_sums, own_sums,
    head, text_head, gains, modulation, activation,
):
    width = embed.shape[1]
    part = weight.shape[2]
    pack = (4, CHUNK + 48, 128)
    grads = (4, 2 * width // COLS, 2 * part)
    rest = (place, out_sum, unpatch_sum, back_sums, own_sums, head, text_head, gains, modulation, activation)
    return pl.pallas_call(
        first_kernel,
        grid_spec=pltpu.PrefetchScalarGridSpec(
            num_scalar_prefetch=2,
            grid=(TOKENS // PAIR,),
            in_specs=[
                lane_block(144, PAIR),
                whole(embed.shape),
                whole(vec.shape),
                held(),
                pl.BlockSpec((3, part, PAIR), lambda t, *_: (0, 0, t)),
                row_block(PAIR, width),
            ]
            + [held()]
            + [whole(value.shape) for value in rest[1:]],
            out_specs=[pl.BlockSpec(pack, lambda t, *_: (0, 0, 0))] * 2
            + [pl.BlockSpec(grads, lambda t, *_: (0, 0, 0))] * 4,
            scratch_shapes=[
                pltpu.VMEM((144, TOKENS), F32),
                pltpu.VMEM((144, width), F32),
                pltpu.VMEM((8, width), F32),
                pltpu.VMEM((8 * CHUNK, 128), BF16),
                pltpu.VMEM((3, part, width), F32),
                pltpu.VMEM((4, width, part), BF16),
            ],
        ),
        out_shape=[jax.ShapeDtypeStruct(pack, BF16)] * 2 + [jax.ShapeDtypeStruct(grads, BF16)] * 4,
        compiler_params=params(58),
        cost_estimate=LIGHT,
        name="first_back",
    )(at, gates, patches, embed, vec, weight, d_raw, d_mid, *rest)


def local(
    latent, condition, caption, cap_len, cotangent, embed_weight, modulate_weight, norm_gains,
    cross_gate, qkv_weight, text_kv_weight, out_weight, gate_up_weight, down_weight, unpatch_weight,
):
    images, _, _, channels = latent.shape
    width = embed_weight.shape[3]
    local_width = qkv_weight.shape[2]
    heads = local_width // HD
    hidden_width = down_weight.shape[0]
    taps = 9 * channels
    row_at = lax.axis_index("row")
    col_at = lax.axis_index("col")
    at = jnp.stack([row_at // 2, row_at % 2, col_at // 4, col_at % 4]).astype(jnp.int32)
    tile = latent.shape[1] * latent.shape[2] * channels

    cond_low = jax.nn.silu(condition.astype(F32)).astype(BF16)
    mod_piece = jnp.dot(cond_low, modulate_weight, preferred_element_type=F32)
    mod_columns = mod_piece.shape[1]
    mod_high = mod_piece.astype(BF16)
    mod_low = (mod_piece - mod_high.astype(F32)).astype(BF16)

    packed = jnp.concatenate(
        [latent.reshape(images, tile), cotangent.reshape(images, tile), mod_high, mod_low], axis=1
    )
    packed = jnp.pad(packed, ((0, 0), (0, 2 * local_width - packed.shape[1])))

    head_piece = jnp.concatenate(
        [
            jnp.concatenate([qkv_weight[0], qkv_weight[1]], axis=1),
            jnp.concatenate([qkv_weight[2], out_weight.T], axis=1),
        ]
    )
    text_piece = jnp.concatenate([text_kv_weight[0], text_kv_weight[1]], axis=1)
    head_pieces = from_col(head_piece, along_y)
    text_pieces = from_col(text_piece, along_z)
    packed = lax.all_to_all(packed, "col", 0, 0, tiled=True)
    packed, *reached = lax.optimization_barrier((packed, *head_pieces, *text_pieces))
    head_pieces, text_pieces = reached[:4], reached[4:]
    packed = send_all(packed, "row")
    patches, cot_taps = image_taps(packed)
    head_pieces = from_col(jnp.stack(head_pieces), along_z)
    text_own = jnp.stack(text_pieces)
    text_beside = [lax.ppermute(text_own, "col", col_pairs(d, 0)) for d in (1, 3)]
    ffn_piece = jnp.concatenate([gate_up_weight[0], gate_up_weight[1], down_weight.T], axis=1)
    ffn_piece, patches, text_own, next_text, last_text, *head_pieces = lax.optimization_barrier(
        (ffn_piece, patches, text_own, *text_beside, *head_pieces)
    )
    ffn_whole = lax.all_gather(ffn_piece, "col", axis=0, tiled=True)
    text_apart = lax.ppermute(text_own, "col", col_pairs(2, 0))
    text_pieces = [text_own, next_text, text_apart, last_text]
    qkv_whole, out_rows = unpack_head(at, head_pieces)
    out_pieces = from_chips(out_rows)

    mod_at = 2 * tile
    modulation = packed[:, :, mod_at : mod_at + mod_columns].astype(F32)
    modulation = modulation + packed[:, :, mod_at + mod_columns : mod_at + 2 * mod_columns].astype(F32)
    modulation = modulation.reshape(4, width)
    attn_gate = jnp.tanh(modulation[1])
    ffn_gate = jnp.tanh(modulation[3])
    vec = jnp.stack(
        [
            norm_gains[0] * (1.0 + modulation[0]),
            norm_gains[1] * attn_gate,
            norm_gains[2] * (1.0 + modulation[2]),
            norm_gains[3] * ffn_gate,
        ]
    )
    vec = jnp.pad(vec, ((0, 4), (0, 0)))
    embed = embed_weight.reshape(taps, width)
    unpatch = unpatch_weight.transpose(0, 1, 3, 2).reshape(taps, width)
    raw = qkv_project(patches, embed, vec, qkv_whole)
    raw = raw.reshape(3, heads, HD, TOKENS)
    caption_rows = caption[0]
    text_raw = text_project(at, text_pieces, caption_rows)
    text_raw = text_raw.reshape(2, heads, HD, caption_rows.shape[0])
    head_gains = lax.dynamic_slice(norm_gains, (4, row_at * local_width), (3, local_width)).reshape(
        3, heads, HD, 1
    )
    head_gates = jnp.tanh(lax.dynamic_slice_in_dim(cross_gate, row_at * heads, heads))
    cap = lax.dynamic_slice_in_dim(cap_len, col_at, 1)
    table = jnp.asarray(rope_tables())
    mixed, lse = attend(raw, text_raw, head_gains, table, cap, head_gates)

    mixed_pieces = from_chips(mixed)
    reached = lax.optimization_barrier((*mixed_pieces, *out_pieces))
    mixed_whole = with_other_core(reached[:4])
    out_whole = with_other_core(reached[4:])
    attn, second, gate_up, hidden, ffn_own, ffn_other = forward(
        at, mixed_whole, out_whole, patches, embed, vec, ffn_whole
    )
    place = tile_places(False)
    cot_own = lax.dynamic_slice_in_dim(cot_taps, row_at * BLOCK, BLOCK, 1)
    d_ffn_own, ffn_out = own_grad(
        to_chips(sum_cores(ffn_own, ffn_other)), cot_own, unpatch, vec
    )
    d_ffn_near = from_chips(d_ffn_own)
    activation_field, unpatch_sum, own_sums = own_block(
        at, ffn_out, attn, patches, cot_taps, embed, unpatch, vec, place
    )
    d_ffn_near = lax.optimization_barrier((*d_ffn_near, activation_field))[:4]
    d_ffn, d_gate_up, d_attn, d_mid, mixed_own, mixed_other, back_sums = backward(
        at, with_other_core(d_ffn_near), ffn_whole, out_whole, gate_up, attn, patches, embed, cot_taps,
        unpatch, vec,
    )
    mixed_near = sum_cores(mixed_own, mixed_other)
    mixed_terms = to_chips(mixed_near)
    text_rows = text_kv_weight.shape[1]
    grads, out_near, out_far = weight_grads(
        after(second, *mixed_near), d_gate_up, d_ffn, hidden, mixed_whole, d_attn, text_rows
    )
    *mixed_terms, grads, out_near, out_far = lax.optimization_barrier(
        (*mixed_terms, grads, out_near, out_far)
    )
    d_mixed = sum(term.astype(F32) for term in mixed_terms).astype(BF16)
    d_mixed = d_mixed.reshape(heads, HD, TOKENS)
    out_near = sum_cores(out_near, out_far)
    out_apart = lax.ppermute(out_near[2], "row", row_pairs_to(2, 0))

    grads, dq_text, d_text_head = text_back(
        raw, text_raw, head_gains, table, lse, d_mixed, cap, head_gates, caption_rows,
        after(grads, *out_near),
    )
    dq_text, grads, out_apart, *out_near = lax.optimization_barrier(
        (dq_text, grads, out_apart, *out_near)
    )
    d_raw, d_head = attend_back(raw, head_gains, table, lse, d_mixed, dq_text)
    out_beside = [lax.ppermute(out_near[d], "row", row_pairs_to(d, 0)) for d in (1, 3)]
    d_raw, *out_terms = lax.optimization_barrier((d_raw, out_near[0], out_apart, *out_beside))
    out_sum = sum(term.astype(F32) for term in out_terms)
    d_raw = d_raw.reshape(3, local_width, TOKENS)
    own_pack, other_pack, *head_parts = first_back(
        at, head_gates, patches, embed, vec, qkv_whole, d_raw, d_mid, place, out_sum, unpatch_sum,
        back_sums, own_sums, d_head, d_text_head, norm_gains, modulation, activation_field,
    )
    beside = [lax.ppermute(head_parts[d], "col", col_pairs_to(0, d)) for d in (1, 3)]

    row_terms = to_chips(sum_cores(own_pack, other_pack))
    row_pack = sum(term.astype(F32) for term in row_terms)
    fields = row_pack[CHUNK : CHUNK + 2 * channels].T.reshape(COLS, 8, 2 * channels)
    mod_sums = row_pack[CHUNK + 2 * channels : CHUNK + 2 * channels + 6].reshape(COLS, 8, 6)
    fields = jnp.concatenate([fields, mod_sums], axis=2).astype(BF16)
    fields = jnp.pad(fields, ((0, 0), (0, 0), (0, 128 - fields.shape[2])))
    shared = row_pack[:CHUNK].astype(BF16).reshape(COLS, CHUNK // COLS, 128)
    col_pack = lax.all_to_all(jnp.concatenate([shared, fields], axis=1), "col", 0, 0)
    col_pack, left, right = lax.optimization_barrier((col_pack, *beside))
    shared = jnp.sum(col_pack[:, : CHUNK // COLS].astype(F32), axis=0)
    shared, apart = lax.optimization_barrier(
        (send_all(shared.astype(BF16), "col"), head_parts[2])
    )
    shared = send_all(shared, "row").reshape(-1, 128)
    apart = lax.ppermute(apart, "col", col_pairs_to(0, 2))
    head_near = sum(term.astype(F32) for term in (head_parts[0], left, apart, right)).astype(BF16)
    shared = shared[: 12 * SHARED].reshape(12, SHARED, 128).astype(F32)
    fields = col_pack[:, CHUNK // COLS :]
    activation = fields[:, :, :channels].reshape(latent.shape)
    latent_grad = fields[:, :, channels : 2 * channels].reshape(latent.shape)
    modulate_grad = lax.dot_general(
        cond_low.astype(F32),
        fields[:, :, 2 * channels : 2 * channels + 6].reshape(images, mod_columns).astype(F32),
        (((0,), (0,)), ((), ())),
        precision=lax.Precision.HIGHEST,
        preferred_element_type=F32,
    )
    embed_grad = shared[:, :taps].transpose(1, 0, 2).reshape(embed_weight.shape)
    unpatch_grad = shared[:, taps : 2 * taps].reshape(12, 3, 3, channels, 128)
    unpatch_grad = unpatch_grad.transpose(1, 2, 0, 4, 3).reshape(unpatch_weight.shape)
    gains_grad = shared[:, 2 * taps : 2 * taps + 7].transpose(1, 0, 2).reshape(7, width)
    gate_grad = shared[0, 2 * taps + 7, :HEADS]

    part = width // COLS
    grads = lax.psum_scatter(
        grads.reshape(-1, 2 * local_width), "col", scatter_dimension=0, tiled=True
    ).astype(F32)
    text_kv_grad = jnp.stack([grads[:text_rows, :local_width], grads[:text_rows, local_width:]])
    ffn_total = jnp.concatenate(
        [grads[first : first + part] for first in range(text_rows, grads.shape[0], part)], axis=1
    )
    gate_up_grad = jnp.stack(
        [ffn_total[:, :hidden_width], ffn_total[:, hidden_width : 2 * hidden_width]]
    )
    down_grad = ffn_total[:, 2 * hidden_width :].T
    head_total = sum(term.astype(F32) for term in along_col(head_near, along_y))
    first, second_half = head_total[:, :local_width], head_total[:, local_width:]
    qkv_grad = jnp.stack([first[:part], second_half[:part], first[part:]])
    out_grad = second_half[part:].T
    return (
        activation, latent_grad, embed_grad, modulate_grad, gains_grad, gate_grad,
        qkv_grad, text_kv_grad, out_grad, gate_up_grad, down_grad, unpatch_grad,
    )


def solution(mesh):
    placed = (
        P(None, "row", "col", None),
        P(),
        P("col", None, None),
        P(),
        P(None, "row", "col", None),
        P(),
        P(None, ("row", "col")),
        P(),
        P(),
        P(None, "col", "row"),
        P(None, "col", "row"),
        P("row", "col"),
        P(None, "col", "row"),
        P("row", "col"),
        P(),
    )
    return jax.shard_map(
        local,
        mesh=mesh,
        in_specs=placed,
        out_specs=(
            P(None, "row", "col", None),
            P(None, "row", "col", None),
            P(),
            P(None, ("row", "col")),
            P(),
            P(),
            P(None, "col", "row"),
            P(None, "col", "row"),
            P("row", "col"),
            P(None, "col", "row"),
            P("row", "col"),
            P(),
        ),
        check_vma=False,
    )
```

profile of v0, /device:TPU:0, one launch (start us, length us, event | category | flops | bytes accessed | tf_op | source)
XLA Modules:
  0.0 414.2 jit_solution(12243381718625031611)
XLA Ops:
  10.9 2.9 collective-permute-start.1
  18.4 3.6 collective-permute-start.4
  24.7 11.1 %all_to_all.32 = bf16[16,2,192]{2,1,0:T(2,128)(2,1)S(1)} all-to-all(bf16[16,2,192]{2,1,0:T(2,128)(2,1)S(1)} %reshape.246), channel_id=1, replica_groups=mesh['row'=8,'col'=16] {'col'}, dimensions={0} | all-to-all | bytes 24576 | tf_op jit(solution)/shard_map/all_to_all | solution.py:1016
  38.1 2.7 collective-permute-start.6
  46.4 4.3 %all-to-all-start.1 = ((bf16[8,16,384]{2,1,0:T(8,128)(2,1)}), bf16[8,16,384]{2,1,0:T(8,128)(2,1)S(1)}, u32[]{:S(2)}, u32[]{:S(2)}) async-start(bf16[8,16,384]{2,1,0:T(8,128)(2,1)} %broadcast_in_dim.9), calls=%async_computation.1 | async-start | bytes 196608 | tf_op jit(solution)/shard_map/all_to_all | solution.py:96
  52.4 4.1 all-to-all-done.1.packed_ref
  58.0 8.5 %collective-permute-done.10.refs_3_ = bf16[4,192,384]{2,1,0:T(8,128)(2,1)} collective-permute-done((bf16[4,192,384]{2,1,0:T(8,128)(2,1)S(1)}, bf16[4,192,384]{2,1,0:T(8,128)(2,1)}, u32[]{:S(2)}, u32[]{:S(2)}) %collective-permute-start.10) | collective-permute-done | bytes 589856 | tf_op jit(solution)/shard_map/ppermute | solution.py:79
  69.6 3.1 unpack_head.1
  74.2 2.8 collective-permute-start.16
  78.7 6.3 %qkv_project.1 = f32[3,192,1024]{2,1,0:T(8,128)S(1)} custom-call(bf16[144,1024]{1,0:T(8,128)(2,1)S(1)} %get-tuple-element.115.patch_ref, bf16[144,1536]{1,0:T(8,128)(2,1)S(1)} %bitcast.146, f32[8,1536]{1,0:T(8,128)S(1)} %select_maximum_fusion.vec_ref, bf16[3,1536,192]{2,1,0:T(8,128)(2,1)S(1)} %get-tuple-element.120.weight_ref), custom_call_target="tpu_custom_call" | custom-call | flops 1 | bytes 1 | tf_op jit(solution)/shard_map/qkv_project/pallas_call | solution.py:512
  85.1 8.4 %collective-permute-done.11.p2_ref = bf16[4,256,384]{2,1,0:T(8,128)(2,1)S(1)} collective-permute-done((bf16[4,256,384]{2,1,0:T(8,128)(2,1)}, bf16[4,256,384]{2,1,0:T(8,128)(2,1)S(1)}, u32[]{:S(2)}, u32[]{:S(2)}) %collective-permute-start.11) | collective-permute-done | bytes 786464 | tf_op jit(solution)/shard_map/ppermute | solution.py:1029
  93.4 3.2 text_project.1
  96.7 10.2 %attend.1 = (bf16[192,1024]{1,0:T(8,128)(2,1)S(1)}, f32[3,8,1024]{2,1,0:T(8,128)S(1)}) custom-call(s32[1]{0:T(128)} %dynamic_slice.14.cap_ref, f32[3]{0:T(128)S(1)} %dynamic-slice_tanh_fusion.gate_ref, f32[3,3,64,1024]{3,2,1,0:T(8,128)S(1)} %bitcast.141, f32[2,3,64,256]{3,2,1,0:T(8,128)S(1)} %bitcast.154, f32[3,3,64,1]{3,2,1,0:T(8,128)S(1)} %reshape.245.gain_ref, ...), custom_call_target="tpu_custom_call" | custom-call | flops 1 | bytes 1 | tf_op jit(solution)/shard_map/attend/pallas_call | solution.py:195
  108.4 2.7 collective-permute-start.13
  112.6 6.4 %collective-permute-done.14 = bf16[192,1024]{1,0:T(8,128)(2,1)S(1)} collective-permute-done((bf16[192,1024]{1,0:T(8,128)(2,1)S(1)}, bf16[192,1024]{1,0:T(8,128)(2,1)S(1)}, u32[]{:S(2)}, u32[]{:S(2)}) %collective-permute-start.14) | collective-permute-done | bytes 393248 | tf_op jit(solution)/shard_map/ppermute | solution.py:49
  119.0 7.3 %collective-permute-done.13 = bf16[192,1024]{1,0:T(8,128)(2,1)S(1)} collective-permute-done((bf16[192,1024]{1,0:T(8,128)(2,1)S(1)}, bf16[192,1024]{1,0:T(8,128)(2,1)S(1)}, u32[]{:S(2)}, u32[]{:S(2)}) %collective-permute-start.13) | collective-permute-done | bytes 393248 | tf_op jit(solution)/shard_map/ppermute | solution.py:49
  129.2 4.3 %collective-permute-done.18.far_ref = bf16[4,192,1024]{2,1,0:T(8,128)(2,1)S(1)} collective-permute-done((bf16[4,192,1024]{2,1,0:T(8,128)(2,1)S(1)}, bf16[4,192,1024]{2,1,0:T(8,128)(2,1)S(1)}, u32[]{:S(2)}, u32[]{:S(2)}) %collective-permute-start.18) | collective-permute-done | bytes 1572896 | tf_op jit(solution)/shard_map/ppermute | solution.py:54
  134.6 19.2 %forward.1 = (bf16[1024,1536]{1,0:T(8,128)(2,1)}, bf16[1024,1536]{1,0:T(8,128)(2,1)}, bf16[1024,1024]{1,0:T(8,128)(2,1)}, bf16[1024,512]{1,0:T(8,128)(2,1)}, bf1...) custom-call(s32[4]{0:T(128)} %copy-done.37, bf16[4,192,1024]{2,1,0:T(8,128)(2,1)} %copy-done.5, ...), custom_call_target="tpu_custom_call" | custom-call | flops 1 | bytes 1 | tf_op jit(solution)/shard_map/forward/pallas_call | solution.py:560
  154.0 3.5 collective-permute-done.20
  157.5 2.9 fusion.7
  160.4 2.3 collective-permute-start.23
  166.0 14.2 %collective-permute-done.23.p3_ref = bf16[128,1536]{1,0:T(8,128)(2,1)} collective-permute-done((bf16[128,1536]{1,0:T(8,128)(2,1)}, bf16[128,1536]{1,0:T(8,128)(2,1)}, u32[]{:S(2)}, u32[]{:S(2)}) %collective-permute-start.23) | collective-permute-done | bytes 393248 | tf_op jit(solution)/shard_map/ppermute | solution.py:67
  180.2 3.7 collective-permute-done.21.p1_ref
  183.9 2.9 own_grad.1
  196.8 11.2 %collective-permute-done.26 = bf16[128,1536]{1,0:T(8,128)(2,1)S(1)} collective-permute-done((bf16[128,1536]{1,0:T(8,128)(2,1)}, bf16[128,1536]{1,0:T(8,128)(2,1)S(1)}, u32[]{:S(2)}, u32[]{:S(2)}) %collective-permute-start.26) | collective-permute-done | bytes 393248 | tf_op jit(solution)/shard_map/ppermute | solution.py:49
  209.0 3.4 collective-permute-done.27.other_ref
  212.4 23.6 %backward.1 = (bf16[1024,1536]{1,0:T(8,128)(2,1)S(1)}, bf16[1024,1024]{1,0:T(8,128)(2,1)S(1)}, bf16[1024,1536]{1,0:T(8,128)(2,1)}, bf16[1024,1536]{1,0:T(8,128)(...) custom-call(s32[4]{0:T(128)S(1)} %copy-done.38, ...), custom_call_target="tpu_custom_call" | custom-call | flops 1 | bytes 1 | tf_op jit(solution)/shard_map/backward/pallas_call | solution.py:726
  237.8 3.3 collective-permute-done.28
  241.8 2.6 collective-permute-start.31
  245.4 14.8 %weight_grads.1 = (bf16[16,640,384]{2,1,0:T(8,128)(2,1)}, bf16[4,192,1536]{2,1,0:T(8,128)(2,1)S(1)}, bf16[4,192,1536]{2,1,0:T(8,128)(2,1)S(1)}) custom-call(bf16[1024,1536]{1,0:T(8,128)(2,1)S(1)} %copy-done.20, bf16[1024,1024]{1,0:T(8,128)(2,1)S(1)} %get-tuple-element.152.d_gate_up_ref, bf16[1024,1536]{1,0:T(8,128)(2,1)} %copy-done.21, ...), custom_call_target="tpu_custom_call" | custom-call | flops 1 | bytes 1 | tf_op jit(solution)/shard_map/weight_grads/pallas_call | solution.py:803
  261.6 3.4 collective-permute-done.29
  265.0 4.5 %collective-permute-done.32 = bf16[4,192,1536]{2,1,0:T(8,128)(2,1)S(1)} collective-permute-done((bf16[4,192,1536]{2,1,0:T(8,128)(2,1)S(1)}, bf16[4,192,1536]{2,1,0:T(8,128)(2,1)S(1)}, u32[]{:S(2)}, u32[]{:S(2)}) %collective-permute-start.32) | collective-permute-done | bytes 2359328 | tf_op jit(solution)/shard_map/ppermute | solution.py:62
  272.0 10.3 %text_back.1 = (bf16[16,640,384]{2,1,0:T(8,128)(2,1)}, f32[3,64,1024]{2,1,0:T(8,128)}, f32[3,8,64]{2,1,0:T(8,128)}) custom-call(s32[1]{0:T(128)} %dynamic_slice.14.cap_ref, f32[3]{0:T(128)} %copy-done.39, f32[3,3,64,1024]{3,2,1,0:T(8,128)} %bitcast.142, f32[2,3,64,256]{3,2,1,0:T(8,128)} %bitcast.155, ...), custom_call_target="tpu_custom_call", output_to_operand_aliasing={{0}: (9, {})} | custom-call | flops 1 | bytes 1 | tf_op jit(solution)/shard_map/text_back/pallas_call | solution.py:271
  282.3 5.0 %collective-permute-done.33 = bf16[192,1536]{1,0:T(8,128)(2,1)S(1)} collective-permute-done((bf16[192,1536]{1,0:T(8,128)(2,1)S(1)}, bf16[192,1536]{1,0:T(8,128)(2,1)S(1)}, u32[]{:S(2)}, u32[]{:S(2)}) %collective-permute-start.33) | collective-permute-done | bytes 589856 | tf_op jit(solution)/shard_map/ppermute | solution.py:1097
  287.4 3.2 collective-permute-start.35
  291.4 14.6 %attend_back.1 = (bf16[3,3,64,1024]{3,2,1,0:T(8,128)(2,1)}, f32[3,8,64]{2,1,0:T(8,128)}) custom-call(f32[3,3,64,1024]{3,2,1,0:T(8,128)} %bitcast.143, f32[3,3,64,1]{3,2,1,0:T(8,128)} %copy-done.17, f32[4,16,1024]{2,1,0:T(8,128)} %constant.82.clone.table_ref, f32[3,8,1024]{2,1,0:T(8,128)} %copy-done.33, bf16[3,64,1024]{2,1,0:T(8,128)(2,1)} %bitcast.164, ...), custom_call_target="tpu_custom_call" | custom-call | flops 1 | bytes 1 | tf_op jit(solution)/shard_map/attend_back/pallas_call | solution.py:344
  306.0 2.4 convert_add_fusion.out_sum_ref
  308.4 19.2 %first_back.1 = (bf16[4,560,128]{2,1,0:T(8,128)(2,1)}, bf16[4,560,128]{2,1,0:T(8,128)(2,1)}, bf16[4,192,384]{2,1,0:T(8,128)(2,1)}, bf16[4,192,384]{2,1,0:T(8,128...) custom-call(s32[4]{0:T(128)} %copy-done.37, f32[3]{0:T(128)} %copy-done.39, ...), custom_call_target="tpu_custom_call" | custom-call | flops 1 | bytes 1 | tf_op jit(solution)/shard_map/first_back/pallas_call | solution.py:948
  331.0 3.2 collective-permute-start.39
  334.3 2.9 collective-permute-start.40
  343.3 6.4 %all-to-all-start.2 = ((bf16[16,40,128]{2,1,0:T(8,128)(2,1)}), bf16[16,40,128]{2,1,0:T(8,128)(2,1)S(1)}, u32[]{:S(2)}, u32[]{:S(2)}) async-start(bf16[16,40,128]{2,1,0:T(8,128)(2,1)} %pad_maximum_fusion.13), calls=%async_computation.2 | async-start | bytes 327680 | tf_op jit(solution)/shard_map/all_to_all | solution.py:1124
  349.7 6.8 %collective-permute-done.40 = bf16[4,192,384]{2,1,0:T(8,128)(2,1)S(1)} collective-permute-done((bf16[4,192,384]{2,1,0:T(8,128)(2,1)}, bf16[4,192,384]{2,1,0:T(8,128)(2,1)S(1)}, u32[]{:S(2)}, u32[]{:S(2)}) %collective-permute-start.40) | collective-permute-done | bytes 589856 | tf_op jit(solution)/shard_map/ppermute | solution.py:1115
  357.8 12.5 %all_to_all.33 = bf16[16,32,128]{2,1,0:T(8,128)(2,1)S(1)} all-to-all(bf16[16,32,128]{2,1,0:T(8,128)(2,1)S(1)} %broadcast_in_dim.10), channel_id=1, replica_groups=mesh['row'=8,'col'=16] {'col'}, dimensions={0} | all-to-all | bytes 262144 | tf_op jit(solution)/shard_map/all_to_all | solution.py:96
  374.5 4.0 all-to-all-start.4
  378.6 7.5 %collective-permute-done.42 = bf16[4,192,384]{2,1,0:T(8,128)(2,1)} collective-permute-done((bf16[4,192,384]{2,1,0:T(8,128)(2,1)}, bf16[4,192,384]{2,1,0:T(8,128)(2,1)}, u32[]{:S(2)}, u32[]{:S(2)}) %collective-permute-start.42) | collective-permute-done | bytes 589856 | tf_op jit(solution)/shard_map/ppermute | solution.py:1131
  388.0 2.7 collective-permute-start.45
  391.9 3.2 collective-permute-done.43
  395.1 2.3 collective-permute-done.44
  (262 shorter events, 85.5 us)
Async XLA Ops:
  9.1 12.8 %collective-permute-start.2 = (bf16[192,384]{1,0:T(8,128)(2,1)S(1)}, bf16[192,384]{1,0:T(8,128)(2,1)S(1)}, u32[]{:S(2)}, u32[]{:S(2)}) collective-permute-start(bf16[192,384]{1,0:T(8,128)(2,1)S(1)} %maximum_maximum_fusion), channel_id=1, source_target_pairs={{12,0},{13,1},{14,2},{15,3},{0,4},{1,5},{2,6},{3,7},{4,8},{5,9},{6... | collective-permute-start | bytes 442376 | tf_op jit(solution)/shard_map/ppermute | solution.py:79
  10.9 25.0 %collective-permute-start.1 = (bf16[192,384]{1,0:T(8,128)(2,1)S(1)}, bf16[192,384]{1,0:T(8,128)(2,1)S(1)}, u32[]{:S(2)}, u32[]{:S(2)}) collective-permute-start(bf16[192,384]{1,0:T(8,128)(2,1)S(1)} %maximum_maximum_fusion), channel_id=1, source_target_pairs={{8,0},{9,1},{10,2},{11,3},{12,4},{13,5},{14,6},{15,7},{0,8},{1,9},... | collective-permute-start | bytes 442376 | tf_op jit(solution)/shard_map/ppermute | solution.py:79
  13.8 22.1 %collective-permute-start = (bf16[192,384]{1,0:T(8,128)(2,1)S(1)}, bf16[192,384]{1,0:T(8,128)(2,1)S(1)}, u32[]{:S(2)}, u32[]{:S(2)}) collective-permute-start(bf16[192,384]{1,0:T(8,128)(2,1)S(1)} %maximum_maximum_fusion), channel_id=1, source_target_pairs={{4,0},{5,1},{6,2},{7,3},{8,4},{9,5},{10,6},{11,7},{12,8},{13,9},{1... | collective-permute-start | bytes 442376 | tf_op jit(solution)/shard_map/ppermute | solution.py:79
  16.4 19.5 %collective-permute-start.5 = (bf16[256,384]{1,0:T(8,128)(2,1)S(1)}, bf16[256,384]{1,0:T(8,128)(2,1)S(1)}, u32[]{:S(2)}, u32[]{:S(2)}) collective-permute-start(bf16[256,384]{1,0:T(8,128)(2,1)S(1)} %pad_maximum_fusion.12), channel_id=1, source_target_pairs={{3,0},{0,1},{1,2},{2,3},{7,4},{4,5},{5,6},{6,7},{11,8},{8,9},{9,10... | collective-permute-start | bytes 589832 | tf_op jit(solution)/shard_map/ppermute | solution.py:79
  18.4 17.5 %collective-permute-start.4 = (bf16[256,384]{1,0:T(8,128)(2,1)S(1)}, bf16[256,384]{1,0:T(8,128)(2,1)S(1)}, u32[]{:S(2)}, u32[]{:S(2)}) collective-permute-start(bf16[256,384]{1,0:T(8,128)(2,1)S(1)} %pad_maximum_fusion.12), channel_id=1, source_target_pairs={{2,0},{3,1},{0,2},{1,3},{6,4},{7,5},{4,6},{5,7},{10,8},{11,9},{8,1... | collective-permute-start | bytes 589832 | tf_op jit(solution)/shard_map/ppermute | solution.py:79
  22.0 13.9 %collective-permute-start.3 = (bf16[256,384]{1,0:T(8,128)(2,1)S(1)}, bf16[256,384]{1,0:T(8,128)(2,1)S(1)}, u32[]{:S(2)}, u32[]{:S(2)}) collective-permute-start(bf16[256,384]{1,0:T(8,128)(2,1)S(1)} %pad_maximum_fusion.12), channel_id=1, source_target_pairs={{1,0},{2,1},{3,2},{0,3},{5,4},{6,5},{7,6},{4,7},{9,8},{10,9},{11,1... | collective-permute-start | bytes 589832 | tf_op jit(solution)/shard_map/ppermute | solution.py:79
  37.5 29.6 %collective-permute-start.7 = (bf16[4,256,384]{2,1,0:T(8,128)(2,1)}, bf16[4,256,384]{2,1,0:T(8,128)(2,1)}, u32[]{:S(2)}, u32[]{:S(2)}) collective-permute-start(bf16[4,256,384]{2,1,0:T(8,128)(2,1)} %pad_maximum_fusion.3.p0_ref), channel_id=1, source_target_pairs={{12,0},{13,1},{14,2},{15,3},{0,4},{1,5},{2,6},{3,7},{4,8},{5,9},{6... | collective-permute-start | bytes 2359304 | tf_op jit(solution)/shard_map/ppermute | solution.py:1023
  38.1 29.1 %collective-permute-start.6 = (bf16[4,256,384]{2,1,0:T(8,128)(2,1)}, bf16[4,256,384]{2,1,0:T(8,128)(2,1)}, u32[]{:S(2)}, u32[]{:S(2)}) collective-permute-start(bf16[4,256,384]{2,1,0:T(8,128)(2,1)} %pad_maximum_fusion.3.p0_ref), channel_id=1, source_target_pairs={{4,0},{5,1},{6,2},{7,3},{8,4},{9,5},{10,6},{11,7},{12,8},{13,9},{1... | collective-permute-start | bytes 2359304 | tf_op jit(solution)/shard_map/ppermute | solution.py:1023
  41.8 24.8 %collective-permute-start.10 = (bf16[4,192,384]{2,1,0:T(8,128)(2,1)S(1)}, bf16[4,192,384]{2,1,0:T(8,128)(2,1)}, u32[]{:S(2)}, u32[]{:S(2)}) collective-permute-start(bf16[4,192,384]{2,1,0:T(8,128)(2,1)S(1)} %pad_maximum_fusion.4.refs_0_), channel_id=1, source_target_pairs={{3,0},{0,1},{1,2},{2,3},{7,4},{4,5},{5,6},{6,7},{11,8},{8,9},{9,10... | collective-permute-start | bytes 1769480 | tf_op jit(solution)/shard_map/ppermute | solution.py:79
  42.4 24.1 %collective-permute-start.9 = (bf16[4,192,384]{2,1,0:T(8,128)(2,1)S(1)}, bf16[4,192,384]{2,1,0:T(8,128)(2,1)}, u32[]{:S(2)}, u32[]{:S(2)}) collective-permute-start(bf16[4,192,384]{2,1,0:T(8,128)(2,1)S(1)} %pad_maximum_fusion.4.refs_0_), channel_id=1, source_target_pairs={{2,0},{3,1},{0,2},{1,3},{6,4},{7,5},{4,6},{5,7},{10,8},{11,9},{8,1... | collective-permute-start | bytes 1769480 | tf_op jit(solution)/shard_map/ppermute | solution.py:79
  44.5 22.7 %collective-permute-start.8 = (bf16[4,192,384]{2,1,0:T(8,128)(2,1)S(1)}, bf16[4,192,384]{2,1,0:T(8,128)(2,1)}, u32[]{:S(2)}, u32[]{:S(2)}) collective-permute-start(bf16[4,192,384]{2,1,0:T(8,128)(2,1)S(1)} %pad_maximum_fusion.4.refs_0_), channel_id=1, source_target_pairs={{1,0},{2,1},{3,2},{0,3},{5,4},{6,5},{7,6},{4,7},{9,8},{10,9},{11,1... | collective-permute-start | bytes 1769480 | tf_op jit(solution)/shard_map/ppermute | solution.py:79
  46.4 10.1 %all-to-all-start.1 = ((bf16[8,16,384]{2,1,0:T(8,128)(2,1)}), bf16[8,16,384]{2,1,0:T(8,128)(2,1)S(1)}, u32[]{:S(2)}, u32[]{:S(2)}) async-start(bf16[8,16,384]{2,1,0:T(8,128)(2,1)} %broadcast_in_dim.9), calls=%async_computation.1 | async-start | bytes 196608 | tf_op jit(solution)/shard_map/all_to_all | solution.py:96
  50.7 84.0 %all-gather.2.cloned.1.call-start = ((), (), s32[]{:S(2)}) async-start(), calls=%async_computation.6 | async-start | bytes 5013504 | tf_op jit(solution)/shard_map/all_gather | solution.py:1028
  67.2 336.1 %reduce-scatter.2.cloned.1.call-start = ((), (), s32[]{:S(2)}) async-start(), calls=%async_computation.7 | async-start | bytes 8355840 | tf_op jit(solution)/shard_map/reduce_scatter | solution.py:1151
  68.6 24.9 %collective-permute-start.11 = (bf16[4,256,384]{2,1,0:T(8,128)(2,1)}, bf16[4,256,384]{2,1,0:T(8,128)(2,1)S(1)}, u32[]{:S(2)}, u32[]{:S(2)}) collective-permute-start(bf16[4,256,384]{2,1,0:T(8,128)(2,1)} %pad_maximum_fusion.3.p0_ref), channel_id=1, source_target_pairs={{8,0},{9,1},{10,2},{11,3},{12,4},{13,5},{14,6},{15,7},{0,8},{1,9},... | collective-permute-start | bytes 2359304 | tf_op jit(solution)/shard_map/ppermute | solution.py:1029
  72.7 38.5 %collective-permute-start.17 = (bf16[192,1536]{1,0:T(8,128)(2,1)S(1)}, bf16[192,1536]{1,0:T(8,128)(2,1)S(1)}, u32[]{:S(2)}, u32[]{:S(2)}) collective-permute-start(bf16[192,1536]{1,0:T(8,128)(2,1)S(1)} %get-tuple-element.131), channel_id=1, source_target_pairs={{96,0},{112,16},{0,32},{16,48},{32,64},{48,80},{64,96},{80,112},{9... | collective-permute-start | bytes 1769480 | tf_op jit(solution)/shard_map/ppermute | solution.py:49
  74.2 38.3 %collective-permute-start.16 = (bf16[192,1536]{1,0:T(8,128)(2,1)S(1)}, bf16[192,1536]{1,0:T(8,128)(2,1)S(1)}, u32[]{:S(2)}, u32[]{:S(2)}) collective-permute-start(bf16[192,1536]{1,0:T(8,128)(2,1)S(1)} %get-tuple-element.131), channel_id=1, source_target_pairs={{64,0},{80,16},{96,32},{112,48},{0,64},{16,80},{32,96},{48,112},{6... | collective-permute-start | bytes 1769480 | tf_op jit(solution)/shard_map/ppermute | solution.py:49
  77.1 35.5 %collective-permute-start.15 = (bf16[192,1536]{1,0:T(8,128)(2,1)S(1)}, bf16[192,1536]{1,0:T(8,128)(2,1)S(1)}, u32[]{:S(2)}, u32[]{:S(2)}) collective-permute-start(bf16[192,1536]{1,0:T(8,128)(2,1)S(1)} %get-tuple-element.131), channel_id=1, source_target_pairs={{32,0},{48,16},{64,32},{80,48},{96,64},{112,80},{0,96},{16,112},{3... | collective-permute-start | bytes 1769480 | tf_op jit(solution)/shard_map/ppermute | solution.py:49
  106.9 12.1 %collective-permute-start.14 = (bf16[192,1024]{1,0:T(8,128)(2,1)S(1)}, bf16[192,1024]{1,0:T(8,128)(2,1)S(1)}, u32[]{:S(2)}, u32[]{:S(2)}) collective-permute-start(bf16[192,1024]{1,0:T(8,128)(2,1)S(1)} %get-tuple-element.127), channel_id=1, source_target_pairs={{96,0},{112,16},{0,32},{16,48},{32,64},{48,80},{64,96},{80,112},{9... | collective-permute-start | bytes 1179656 | tf_op jit(solution)/shard_map/ppermute | solution.py:49
  108.4 17.9 %collective-permute-start.13 = (bf16[192,1024]{1,0:T(8,128)(2,1)S(1)}, bf16[192,1024]{1,0:T(8,128)(2,1)S(1)}, u32[]{:S(2)}, u32[]{:S(2)}) collective-permute-start(bf16[192,1024]{1,0:T(8,128)(2,1)S(1)} %get-tuple-element.127), channel_id=1, source_target_pairs={{64,0},{80,16},{96,32},{112,48},{0,64},{16,80},{32,96},{48,112},{6... | collective-permute-start | bytes 1179656 | tf_op jit(solution)/shard_map/ppermute | solution.py:49
  111.1 15.2 %collective-permute-start.12 = (bf16[192,1024]{1,0:T(8,128)(2,1)S(1)}, bf16[192,1024]{1,0:T(8,128)(2,1)S(1)}, u32[]{:S(2)}, u32[]{:S(2)}) collective-permute-start(bf16[192,1024]{1,0:T(8,128)(2,1)S(1)} %get-tuple-element.127), channel_id=1, source_target_pairs={{32,0},{48,16},{64,32},{80,48},{96,64},{112,80},{0,96},{16,112},{3... | collective-permute-start | bytes 1179656 | tf_op jit(solution)/shard_map/ppermute | solution.py:49
  126.6 8.0 %collective-permute-start.19 = (bf16[4,192,1536]{2,1,0:T(8,128)(2,1)S(1)}, bf16[4,192,1536]{2,1,0:T(8,128)(2,1)}, u32[]{:S(2)}, u32[]{:S(2)}) collective-permute-start(bf16[4,192,1536]{2,1,0:T(8,128)(2,1)S(1)} %pad_maximum_fusion.out_near_ref), channel_id=1, source_target_pairs={{16,0},{0,16},{48,32},{32,48},{80,64},{64,80},{112,96},{96,112},{1... | collective-permute-start | bytes 7077896 | tf_op jit(solution)/shard_map/ppermute | solution.py:54
  128.0 5.5 %collective-permute-start.18 = (bf16[4,192,1024]{2,1,0:T(8,128)(2,1)S(1)}, bf16[4,192,1024]{2,1,0:T(8,128)(2,1)S(1)}, u32[]{:S(2)}, u32[]{:S(2)}) collective-permute-start(bf16[4,192,1024]{2,1,0:T(8,128)(2,1)S(1)} %pad_maximum_fusion.1.near_ref), channel_id=1, source_target_pairs={{16,0},{0,16},{48,32},{32,48},{80,64},{64,80},{112,96},{96,112},{1... | collective-permute-start | bytes 4718600 | tf_op jit(solution)/shard_map/ppermute | solution.py:54
  153.8 3.7 collective-permute-start.20
  160.4 19.8 %collective-permute-start.23 = (bf16[128,1536]{1,0:T(8,128)(2,1)}, bf16[128,1536]{1,0:T(8,128)(2,1)}, u32[]{:S(2)}, u32[]{:S(2)}) collective-permute-start(bf16[128,1536]{1,0:T(8,128)(2,1)} %get-tuple-element.256), channel_id=1, source_target_pairs={{0,96},{16,112},{32,0},{48,16},{64,32},{80,48},{96,64},{112,80},{1... | collective-permute-start | bytes 1179656 | tf_op jit(solution)/shard_map/ppermute | solution.py:67
  162.7 17.5 %collective-permute-start.22 = (bf16[128,1536]{1,0:T(8,128)(2,1)}, bf16[128,1536]{1,0:T(8,128)(2,1)}, u32[]{:S(2)}, u32[]{:S(2)}) collective-permute-start(bf16[128,1536]{1,0:T(8,128)(2,1)} %get-tuple-element.257), channel_id=1, source_target_pairs={{0,64},{16,80},{32,96},{48,112},{64,0},{80,16},{96,32},{112,48},{1... | collective-permute-start | bytes 1179656 | tf_op jit(solution)/shard_map/ppermute | solution.py:67
  163.9 20.0 %collective-permute-start.21 = (bf16[128,1536]{1,0:T(8,128)(2,1)}, bf16[128,1536]{1,0:T(8,128)(2,1)}, u32[]{:S(2)}, u32[]{:S(2)}) collective-permute-start(bf16[128,1536]{1,0:T(8,128)(2,1)} %get-tuple-element.258), channel_id=1, source_target_pairs={{0,32},{16,48},{32,64},{48,80},{64,96},{80,112},{96,0},{112,16},{1... | collective-permute-start | bytes 1179656 | tf_op jit(solution)/shard_map/ppermute | solution.py:67
  186.8 21.3 %collective-permute-start.26 = (bf16[128,1536]{1,0:T(8,128)(2,1)}, bf16[128,1536]{1,0:T(8,128)(2,1)S(1)}, u32[]{:S(2)}, u32[]{:S(2)}) collective-permute-start(bf16[128,1536]{1,0:T(8,128)(2,1)} %get-tuple-element.143), channel_id=1, source_target_pairs={{96,0},{112,16},{0,32},{16,48},{32,64},{48,80},{64,96},{80,112},{9... | collective-permute-start | bytes 1179656 | tf_op jit(solution)/shard_map/ppermute | solution.py:49
  187.2 20.9 %collective-permute-start.25 = (bf16[128,1536]{1,0:T(8,128)(2,1)}, bf16[128,1536]{1,0:T(8,128)(2,1)S(1)}, u32[]{:S(2)}, u32[]{:S(2)}) collective-permute-start(bf16[128,1536]{1,0:T(8,128)(2,1)} %get-tuple-element.143), channel_id=1, source_target_pairs={{64,0},{80,16},{96,32},{112,48},{0,64},{16,80},{32,96},{48,112},{6... | collective-permute-start | bytes 1179656 | tf_op jit(solution)/shard_map/ppermute | solution.py:49
  189.2 19.4 %collective-permute-start.24 = (bf16[128,1536]{1,0:T(8,128)(2,1)}, bf16[128,1536]{1,0:T(8,128)(2,1)S(1)}, u32[]{:S(2)}, u32[]{:S(2)}) collective-permute-start(bf16[128,1536]{1,0:T(8,128)(2,1)} %get-tuple-element.143), channel_id=1, source_target_pairs={{32,0},{48,16},{64,32},{80,48},{96,64},{112,80},{0,96},{16,112},{3... | collective-permute-start | bytes 1179656 | tf_op jit(solution)/shard_map/ppermute | solution.py:49
  241.8 19.8 %collective-permute-start.31 = (bf16[192,1024]{1,0:T(8,128)(2,1)S(1)}, bf16[192,1024]{1,0:T(8,128)(2,1)S(1)}, u32[]{:S(2)}, u32[]{:S(2)}) collective-permute-start(bf16[192,1024]{1,0:T(8,128)(2,1)S(1)} %get-tuple-element.252), channel_id=1, source_target_pairs={{0,96},{16,112},{32,0},{48,16},{64,32},{80,48},{96,64},{112,80},{1... | collective-permute-start | bytes 1179656 | tf_op jit(solution)/shard_map/ppermute | solution.py:67
  244.5 17.1 %collective-permute-start.30 = (bf16[192,1024]{1,0:T(8,128)(2,1)S(1)}, bf16[192,1024]{1,0:T(8,128)(2,1)S(1)}, u32[]{:S(2)}, u32[]{:S(2)}) collective-permute-start(bf16[192,1024]{1,0:T(8,128)(2,1)S(1)} %get-tuple-element.253), channel_id=1, source_target_pairs={{0,64},{16,80},{32,96},{48,112},{64,0},{80,16},{96,32},{112,48},{1... | collective-permute-start | bytes 1179656 | tf_op jit(solution)/shard_map/ppermute | solution.py:67
  244.5 20.5 %collective-permute-start.29 = (bf16[192,1024]{1,0:T(8,128)(2,1)S(1)}, bf16[192,1024]{1,0:T(8,128)(2,1)S(1)}, u32[]{:S(2)}, u32[]{:S(2)}) collective-permute-start(bf16[192,1024]{1,0:T(8,128)(2,1)S(1)} %get-tuple-element.254), channel_id=1, source_target_pairs={{0,32},{16,48},{32,64},{48,80},{64,96},{80,112},{96,0},{112,16},{1... | collective-permute-start | bytes 1179656 | tf_op jit(solution)/shard_map/ppermute | solution.py:67
  265.0 4.5 %collective-permute-start.32 = (bf16[4,192,1536]{2,1,0:T(8,128)(2,1)S(1)}, bf16[4,192,1536]{2,1,0:T(8,128)(2,1)S(1)}, u32[]{:S(2)}, u32[]{:S(2)}) collective-permute-start(bf16[4,192,1536]{2,1,0:T(8,128)(2,1)S(1)} %get-tuple-element.165), channel_id=1, source_target_pairs={{16,0},{0,16},{48,32},{32,48},{80,64},{64,80},{112,96},{96,112},{1... | collective-permute-start | bytes 7077896 | tf_op jit(solution)/shard_map/ppermute | solution.py:62
  270.2 17.1 %collective-permute-start.33 = (bf16[192,1536]{1,0:T(8,128)(2,1)S(1)}, bf16[192,1536]{1,0:T(8,128)(2,1)S(1)}, u32[]{:S(2)}, u32[]{:S(2)}) collective-permute-start(bf16[192,1536]{1,0:T(8,128)(2,1)S(1)} %get-tuple-element.249), channel_id=1, source_target_pairs={{0,64},{16,80},{32,96},{48,112},{64,0},{80,16},{96,32},{112,48},{1... | collective-permute-start | bytes 1769480 | tf_op jit(solution)/shard_map/ppermute | solution.py:1097
  287.3 18.6 %collective-permute-start.34 = (bf16[192,1536]{1,0:T(8,128)(2,1)S(1)}, bf16[192,1536]{1,0:T(8,128)(2,1)S(1)}, u32[]{:S(2)}, u32[]{:S(2)}) collective-permute-start(bf16[192,1536]{1,0:T(8,128)(2,1)S(1)} %get-tuple-element.173), channel_id=1, source_target_pairs={{0,32},{16,48},{32,64},{48,80},{64,96},{80,112},{96,0},{112,16},{1... | collective-permute-start | bytes 1769480 | tf_op jit(solution)/shard_map/ppermute | solution.py:1107
  287.4 18.5 %collective-permute-start.35 = (bf16[192,1536]{1,0:T(8,128)(2,1)S(1)}, bf16[192,1536]{1,0:T(8,128)(2,1)}, u32[]{:S(2)}, u32[]{:S(2)}) collective-permute-start(bf16[192,1536]{1,0:T(8,128)(2,1)S(1)} %get-tuple-element.174), channel_id=1, source_target_pairs={{0,96},{16,112},{32,0},{48,16},{64,32},{80,48},{96,64},{112,80},{1... | collective-permute-start | bytes 1769480 | tf_op jit(solution)/shard_map/ppermute | solution.py:1107
  331.0 8.3 %collective-permute-start.37 = (bf16[560,128]{1,0:T(8,128)(2,1)S(1)}, bf16[560,128]{1,0:T(8,128)(2,1)S(1)}, u32[]{:S(2)}, u32[]{:S(2)}) collective-permute-start(bf16[560,128]{1,0:T(8,128)(2,1)S(1)} %get-tuple-element.260), channel_id=1, source_target_pairs={{0,32},{16,48},{32,64},{48,80},{64,96},{80,112},{96,0},{112,16},{1... | collective-permute-start | bytes 430088 | tf_op jit(solution)/shard_map/ppermute | solution.py:67
  331.0 9.4 %collective-permute-start.39 = (bf16[560,128]{1,0:T(8,128)(2,1)S(1)}, bf16[560,128]{1,0:T(8,128)(2,1)S(1)}, u32[]{:S(2)}, u32[]{:S(2)}) collective-permute-start(bf16[560,128]{1,0:T(8,128)(2,1)S(1)} %get-tuple-element.261), channel_id=1, source_target_pairs={{0,96},{16,112},{32,0},{48,16},{64,32},{80,48},{96,64},{112,80},{1... | collective-permute-start | bytes 430088 | tf_op jit(solution)/shard_map/ppermute | solution.py:67
  334.3 6.9 %collective-permute-start.38 = (bf16[560,128]{1,0:T(8,128)(2,1)S(1)}, bf16[560,128]{1,0:T(8,128)(2,1)S(1)}, u32[]{:S(2)}, u32[]{:S(2)}) collective-permute-start(bf16[560,128]{1,0:T(8,128)(2,1)S(1)} %get-tuple-element.262), channel_id=1, source_target_pairs={{0,64},{16,80},{32,96},{48,112},{64,0},{80,16},{96,32},{112,48},{1... | collective-permute-start | bytes 430088 | tf_op jit(solution)/shard_map/ppermute | solution.py:67
  334.3 22.2 %collective-permute-start.40 = (bf16[4,192,384]{2,1,0:T(8,128)(2,1)}, bf16[4,192,384]{2,1,0:T(8,128)(2,1)S(1)}, u32[]{:S(2)}, u32[]{:S(2)}) collective-permute-start(bf16[4,192,384]{2,1,0:T(8,128)(2,1)} %get-tuple-element.188), channel_id=1, source_target_pairs={{0,1},{1,2},{2,3},{3,0},{4,5},{5,6},{6,7},{7,4},{8,9},{9,10},{10,1... | collective-permute-start | bytes 1769480 | tf_op jit(solution)/shard_map/ppermute | solution.py:1115
  337.1 19.3 %collective-permute-start.41 = (bf16[4,192,384]{2,1,0:T(8,128)(2,1)}, bf16[4,192,384]{2,1,0:T(8,128)(2,1)S(1)}, u32[]{:S(2)}, u32[]{:S(2)}) collective-permute-start(bf16[4,192,384]{2,1,0:T(8,128)(2,1)} %get-tuple-element.189), channel_id=1, source_target_pairs={{0,3},{1,0},{2,1},{3,2},{4,7},{5,4},{6,5},{7,6},{8,11},{9,8},{10,9... | collective-permute-start | bytes 1769480 | tf_op jit(solution)/shard_map/ppermute | solution.py:1115
  343.3 14.5 %all-to-all-start.2 = ((bf16[16,40,128]{2,1,0:T(8,128)(2,1)}), bf16[16,40,128]{2,1,0:T(8,128)(2,1)S(1)}, u32[]{:S(2)}, u32[]{:S(2)}) async-start(bf16[16,40,128]{2,1,0:T(8,128)(2,1)} %pad_maximum_fusion.13), calls=%async_computation.2 | async-start | bytes 327680 | tf_op jit(solution)/shard_map/all_to_all | solution.py:1124
  370.3 15.7 %collective-permute-start.42 = (bf16[4,192,384]{2,1,0:T(8,128)(2,1)}, bf16[4,192,384]{2,1,0:T(8,128)(2,1)}, u32[]{:S(2)}, u32[]{:S(2)}) collective-permute-start(bf16[4,192,384]{2,1,0:T(8,128)(2,1)} %get-tuple-element.195), channel_id=1, source_target_pairs={{0,2},{1,3},{2,0},{3,1},{4,6},{5,7},{6,4},{7,5},{8,10},{9,11},{10,... | collective-permute-start | bytes 1769480 | tf_op jit(solution)/shard_map/ppermute | solution.py:1131
  374.5 24.6 %all-to-all-start.4 = ((bf16[8,16,32,128]{3,2,1,0:T(8,128)(2,1)}), bf16[8,16,32,128]{3,2,1,0:T(8,128)(2,1)S(1)}, u32[]{:S(2)}, u32[]{:S(2)}) async-start(bf16[8,16,32,128]{3,2,1,0:T(8,128)(2,1)} %broadcast_in_dim.11), calls=%async_computation.4 | async-start | bytes 2097152 | tf_op jit(solution)/shard_map/all_to_all | solution.py:96
  387.5 7.6 %collective-permute-start.43 = (bf16[192,384]{1,0:T(8,128)(2,1)S(1)}, bf16[192,384]{1,0:T(8,128)(2,1)S(1)}, u32[]{:S(2)}, u32[]{:S(2)}) collective-permute-start(bf16[192,384]{1,0:T(8,128)(2,1)S(1)} %get-tuple-element.265), channel_id=1, source_target_pairs={{0,4},{1,5},{2,6},{3,7},{4,8},{5,9},{6,10},{7,11},{8,12},{9,13},{1... | collective-permute-start | bytes 442376 | tf_op jit(solution)/shard_map/ppermute | solution.py:91
  388.0 7.1 %collective-permute-start.45 = (bf16[192,384]{1,0:T(8,128)(2,1)S(1)}, bf16[192,384]{1,0:T(8,128)(2,1)S(1)}, u32[]{:S(2)}, u32[]{:S(2)}) collective-permute-start(bf16[192,384]{1,0:T(8,128)(2,1)S(1)} %get-tuple-element.266), channel_id=1, source_target_pairs={{0,12},{1,13},{2,14},{3,15},{4,0},{5,1},{6,2},{7,3},{8,4},{9,5},{1... | collective-permute-start | bytes 442376 | tf_op jit(solution)/shard_map/ppermute | solution.py:91
  390.8 6.6 %collective-permute-start.44 = (bf16[192,384]{1,0:T(8,128)(2,1)S(1)}, bf16[192,384]{1,0:T(8,128)(2,1)S(1)}, u32[]{:S(2)}, u32[]{:S(2)}) collective-permute-start(bf16[192,384]{1,0:T(8,128)(2,1)S(1)} %get-tuple-element.267), channel_id=1, source_target_pairs={{0,8},{1,9},{2,10},{3,11},{4,12},{5,13},{6,14},{7,15},{8,0},{9,1},... | collective-permute-start | bytes 442376 | tf_op jit(solution)/shard_map/ppermute | solution.py:91
  (57 other events, 730.2 us)
Sparse Core Ops, SparseCore 0:
  67.3 55.4 all-gather.1
  287.5 87.1 reduce-scatter.1
where the time goes:
time: 422 us; the launch traced here: 414 us
  Pallas kernels  130 us (31%)
  waiting for transfers between devices  119 us (28%)
  starting transfers between devices  76.7 us (18%)
  local copies, waits for them, and re-layouts  27.3 us (6%)
  blocking collectives  23.6 us (6%)
  other arithmetic  21.2 us (5%)
  between operations  15.1 us (4%)
    ppermute x9, waiting for transfers between devices, from_chips(): lax.ppermute(piece, 'row', row_pairs(d, 0))  25.6 us
    ppermute x9, waiting for transfers between devices, to_chips(): lax.ppermute(near[d], 'row', row_pairs_to(d, 0))  24.4 us
    pallas_call x1, Pallas kernels, backward(): pl.pallas_call(backward_kernel, grid_spec=pltpu.PrefetchScalarGridSpec(nu...  23.6 us
    pallas_call x1, Pallas kernels, first_back(): pl.pallas_call(first_kernel, grid_spec=pltpu.PrefetchScalarGridSpec(num_s...  19.2 us
    pallas_call x1, Pallas kernels, forward(): pl.pallas_call(forward_kernel, grid_spec=pltpu.PrefetchScalarGridSpec(num...  19.2 us
    ppermute x9, starting transfers between devices, from_col(): lax.ppermute(piece, 'col', col_pairs(*step(d)))  16.5 us
    ppermute x9, starting transfers between devices, from_chips(): lax.ppermute(piece, 'row', row_pairs(d, 0))  15.8 us
    pallas_call x1, Pallas kernels, weight_grads(): pl.pallas_call(weight_kernel, grid=(4,), in_specs=[lane_block(TOKENS, wid...  14.8 us
  transfers between devices with their start and end apart: 51, of which 26 were waited for; matrix products, arithmetic and copies ran while one was open for 7% of the time, Pallas kernels for 20%

commit v1 on v0

--- a/solution.py
+++ b/solution.py
@@ -1159,7 +1159,20 @@
         [ffn_total[:, :hidden_width], ffn_total[:, hidden_width : 2 * hidden_width]]
     )
     down_grad = ffn_total[:, 2 * hidden_width :].T
-    head_total = sum(term.astype(F32) for term in along_col(head_near, along_y))
+    head_terms, others = lax.optimization_barrier(
+        (
+            along_col(head_near, along_y),
+            (
+                activation, latent_grad, embed_grad, modulate_grad, gains_grad, gate_grad,
+                text_kv_grad, gate_up_grad, down_grad, unpatch_grad,
+            ),
+        )
+    )
+    (
+        activation, latent_grad, embed_grad, modulate_grad, gains_grad, gate_grad,
+        text_kv_grad, gate_up_grad, down_grad, unpatch_grad,
+    ) = others
+    head_total = sum(term.astype(F32) for term in head_terms)
     first, second_half = head_total[:, :local_width], head_total[:, local_width:]
     qkv_grad = jnp.stack([first[:part], second_half[:part], first[part:]])
     out_grad = second_half[part:].T

time: 422 us -> 420 us (level)
    ppermute x3, waiting for transfers between devices: 5.53 us -> 0.01 us  [along_col(): lax.ppermute(parts[d], 'col', col_pairs_to(*step(d)))]
  transfers between devices with their start and end apart: 51 -> 51, of which waited for: 26 -> 25; matrix products, arithmetic and copies ran while one was open for 7% -> 7% of each run, Pallas kernels for 20% -> 21%
where the time goes in v1:
time: 420 us; the launch traced here: 412 us
  Pallas kernels  131 us (31%)
  waiting for transfers between devices  115 us (27%)
  starting transfers between devices  76.4 us (18%)
  local copies, waits for them, and re-layouts  28 us (7%)
  blocking collectives  23.5 us (6%)
  other arithmetic  22.3 us (5%)
  between operations  15.2 us (4%)
    ppermute x9, waiting for transfers between devices, from_chips(): lax.ppermute(piece, 'row', row_pairs(d, 0))  25.5 us
    ppermute x9, waiting for transfers between devices, to_chips(): lax.ppermute(near[d], 'row', row_pairs_to(d, 0))  24.3 us
    pallas_call x1, Pallas kernels, backward(): pl.pallas_call(backward_kernel, grid_spec=pltpu.PrefetchScalarGridSpec(nu...  23.6 us
    pallas_call x1, Pallas kernels, forward(): pl.pallas_call(forward_kernel, grid_spec=pltpu.PrefetchScalarGridSpec(num...  19.2 us
    pallas_call x1, Pallas kernels, first_back(): pl.pallas_call(first_kernel, grid_spec=pltpu.PrefetchScalarGridSpec(num_s...  19.1 us
    ppermute x9, starting transfers between devices, from_col(): lax.ppermute(piece, 'col', col_pairs(*step(d)))  16.5 us
    ppermute x9, starting transfers between devices, from_chips(): lax.ppermute(piece, 'row', row_pairs(d, 0))  15.8 us
    pallas_call x1, Pallas kernels, weight_grads(): pl.pallas_call(weight_kernel, grid=(4,), in_specs=[lane_block(TOKENS, wid...  14.9 us
  transfers between devices with their start and end apart: 51, of which 25 were waited for; matrix products, arithmetic and copies ran while one was open for 7% of the time, Pallas kernels for 21%

profile of v1, /device:TPU:0, one launch (start us, length us, event | category | flops | bytes accessed | tf_op | source)
XLA Modules:
  0.0 411.6 jit_solution(13395552469503506578)
XLA Ops:
  10.9 2.9 collective-permute-start.1
  18.4 3.6 collective-permute-start.4
  24.7 11.1 %all_to_all.32 = bf16[16,2,192]{2,1,0:T(2,128)(2,1)S(1)} all-to-all(bf16[16,2,192]{2,1,0:T(2,128)(2,1)S(1)} %reshape.243), channel_id=1, replica_groups=mesh['row'=8,'col'=16] {'col'}, dimensions={0} | all-to-all | bytes 24576 | tf_op jit(solution)/shard_map/all_to_all | solution.py:1016
  38.1 2.7 collective-permute-start.6
  46.4 4.3 %all-to-all-start.1 = ((bf16[8,16,384]{2,1,0:T(8,128)(2,1)}), bf16[8,16,384]{2,1,0:T(8,128)(2,1)S(1)}, u32[]{:S(2)}, u32[]{:S(2)}) async-start(bf16[8,16,384]{2,1,0:T(8,128)(2,1)} %broadcast_in_dim.9), calls=%async_computation.1 | async-start | bytes 196608 | tf_op jit(solution)/shard_map/all_to_all | solution.py:96
  52.4 4.1 all-to-all-done.1.packed_ref
  58.1 8.5 %collective-permute-done.10.refs_3_ = bf16[4,192,384]{2,1,0:T(8,128)(2,1)} collective-permute-done((bf16[4,192,384]{2,1,0:T(8,128)(2,1)S(1)}, bf16[4,192,384]{2,1,0:T(8,128)(2,1)}, u32[]{:S(2)}, u32[]{:S(2)}) %collective-permute-start.10) | collective-permute-done | bytes 589856 | tf_op jit(solution)/shard_map/ppermute | solution.py:79
  69.6 3.1 unpack_head.1
  74.2 2.8 collective-permute-start.16
  78.7 6.3 %qkv_project.1 = f32[3,192,1024]{2,1,0:T(8,128)S(1)} custom-call(bf16[144,1024]{1,0:T(8,128)(2,1)S(1)} %get-tuple-element.129.patch_ref, bf16[144,1536]{1,0:T(8,128)(2,1)S(1)} %bitcast.143, f32[8,1536]{1,0:T(8,128)S(1)} %select_maximum_fusion.vec_ref, bf16[3,1536,192]{2,1,0:T(8,128)(2,1)S(1)} %get-tuple-element.134.weight_ref), custom_call_target="tpu_custom_call" | custom-call | flops 1 | bytes 1 | tf_op jit(solution)/shard_map/qkv_project/pallas_call | solution.py:512
  85.1 8.4 %collective-permute-done.11.p2_ref = bf16[4,256,384]{2,1,0:T(8,128)(2,1)S(1)} collective-permute-done((bf16[4,256,384]{2,1,0:T(8,128)(2,1)}, bf16[4,256,384]{2,1,0:T(8,128)(2,1)S(1)}, u32[]{:S(2)}, u32[]{:S(2)}) %collective-permute-start.11) | collective-permute-done | bytes 786464 | tf_op jit(solution)/shard_map/ppermute | solution.py:1029
  93.4 3.2 text_project.1
  96.7 10.2 %attend.1 = (bf16[192,1024]{1,0:T(8,128)(2,1)S(1)}, f32[3,8,1024]{2,1,0:T(8,128)S(1)}) custom-call(s32[1]{0:T(128)} %dynamic_slice.14.cap_ref, f32[3]{0:T(128)S(1)} %dynamic-slice_tanh_fusion.gate_ref, f32[3,3,64,1024]{3,2,1,0:T(8,128)S(1)} %bitcast.138, f32[2,3,64,256]{3,2,1,0:T(8,128)S(1)} %bitcast.151, f32[3,3,64,1]{3,2,1,0:T(8,128)S(1)} %reshape.242.gain_ref, ...), custom_call_target="tpu_custom_call" | custom-call | flops 1 | bytes 1 | tf_op jit(solution)/shard_map/attend/pallas_call | solution.py:195
  108.4 2.7 collective-permute-start.13
  112.6 6.4 %collective-permute-done.14 = bf16[192,1024]{1,0:T(8,128)(2,1)S(1)} collective-permute-done((bf16[192,1024]{1,0:T(8,128)(2,1)S(1)}, bf16[192,1024]{1,0:T(8,128)(2,1)S(1)}, u32[]{:S(2)}, u32[]{:S(2)}) %collective-permute-start.14) | collective-permute-done | bytes 393248 | tf_op jit(solution)/shard_map/ppermute | solution.py:49
  119.0 7.3 %collective-permute-done.13 = bf16[192,1024]{1,0:T(8,128)(2,1)S(1)} collective-permute-done((bf16[192,1024]{1,0:T(8,128)(2,1)S(1)}, bf16[192,1024]{1,0:T(8,128)(2,1)S(1)}, u32[]{:S(2)}, u32[]{:S(2)}) %collective-permute-start.13) | collective-permute-done | bytes 393248 | tf_op jit(solution)/shard_map/ppermute | solution.py:49
  129.2 4.3 %collective-permute-done.18.far_ref = bf16[4,192,1024]{2,1,0:T(8,128)(2,1)S(1)} collective-permute-done((bf16[4,192,1024]{2,1,0:T(8,128)(2,1)S(1)}, bf16[4,192,1024]{2,1,0:T(8,128)(2,1)S(1)}, u32[]{:S(2)}, u32[]{:S(2)}) %collective-permute-start.18) | collective-permute-done | bytes 1572896 | tf_op jit(solution)/shard_map/ppermute | solution.py:54
  134.6 19.2 %forward.1 = (bf16[1024,1536]{1,0:T(8,128)(2,1)}, bf16[1024,1536]{1,0:T(8,128)(2,1)}, bf16[1024,1024]{1,0:T(8,128)(2,1)}, bf16[1024,512]{1,0:T(8,128)(2,1)}, bf1...) custom-call(s32[4]{0:T(128)} %copy-done.37, bf16[4,192,1024]{2,1,0:T(8,128)(2,1)} %copy-done.5, ...), custom_call_target="tpu_custom_call" | custom-call | flops 1 | bytes 1 | tf_op jit(solution)/shard_map/forward/pallas_call | solution.py:560
  154.0 3.5 collective-permute-done.20
  157.5 2.9 fusion.7
  160.5 2.3 collective-permute-start.23
  166.0 14.2 %collective-permute-done.23.p3_ref = bf16[128,1536]{1,0:T(8,128)(2,1)} collective-permute-done((bf16[128,1536]{1,0:T(8,128)(2,1)}, bf16[128,1536]{1,0:T(8,128)(2,1)}, u32[]{:S(2)}, u32[]{:S(2)}) %collective-permute-start.23) | collective-permute-done | bytes 393248 | tf_op jit(solution)/shard_map/ppermute | solution.py:67
  180.2 3.7 collective-permute-done.21.p1_ref
  183.8 2.9 own_grad.1
  194.7 2.2 own_block.1
  196.9 11.2 %collective-permute-done.26 = bf16[128,1536]{1,0:T(8,128)(2,1)S(1)} collective-permute-done((bf16[128,1536]{1,0:T(8,128)(2,1)}, bf16[128,1536]{1,0:T(8,128)(2,1)S(1)}, u32[]{:S(2)}, u32[]{:S(2)}) %collective-permute-start.26) | collective-permute-done | bytes 393248 | tf_op jit(solution)/shard_map/ppermute | solution.py:49
  209.0 3.4 collective-permute-done.27.other_ref
  212.4 23.6 %backward.1 = (bf16[1024,1536]{1,0:T(8,128)(2,1)S(1)}, bf16[1024,1024]{1,0:T(8,128)(2,1)S(1)}, bf16[1024,1536]{1,0:T(8,128)(2,1)}, bf16[1024,1536]{1,0:T(8,128)(...) custom-call(s32[4]{0:T(128)S(1)} %copy-done.38, ...), custom_call_target="tpu_custom_call" | custom-call | flops 1 | bytes 1 | tf_op jit(solution)/shard_map/backward/pallas_call | solution.py:726
  237.8 3.3 collective-permute-done.28
  241.8 2.7 collective-permute-start.31
  245.5 14.9 %weight_grads.1 = (bf16[16,640,384]{2,1,0:T(8,128)(2,1)}, bf16[4,192,1536]{2,1,0:T(8,128)(2,1)S(1)}, bf16[4,192,1536]{2,1,0:T(8,128)(2,1)S(1)}) custom-call(bf16[1024,1536]{1,0:T(8,128)(2,1)S(1)} %copy-done.20, bf16[1024,1024]{1,0:T(8,128)(2,1)S(1)} %get-tuple-element.166.d_gate_up_ref, bf16[1024,1536]{1,0:T(8,128)(2,1)} %copy-done.21, ...), custom_call_target="tpu_custom_call" | custom-call | flops 1 | bytes 1 | tf_op jit(solution)/shard_map/weight_grads/pallas_call | solution.py:803
  261.6 3.4 collective-permute-done.29
  265.0 4.5 %collective-permute-done.32 = bf16[4,192,1536]{2,1,0:T(8,128)(2,1)S(1)} collective-permute-done((bf16[4,192,1536]{2,1,0:T(8,128)(2,1)S(1)}, bf16[4,192,1536]{2,1,0:T(8,128)(2,1)S(1)}, u32[]{:S(2)}, u32[]{:S(2)}) %collective-permute-start.32) | collective-permute-done | bytes 2359328 | tf_op jit(solution)/shard_map/ppermute | solution.py:62
  272.1 10.3 %text_back.1 = (bf16[16,640,384]{2,1,0:T(8,128)(2,1)}, f32[3,64,1024]{2,1,0:T(8,128)}, f32[3,8,64]{2,1,0:T(8,128)}) custom-call(s32[1]{0:T(128)} %dynamic_slice.14.cap_ref, f32[3]{0:T(128)} %copy-done.39, f32[3,3,64,1024]{3,2,1,0:T(8,128)} %bitcast.139, f32[2,3,64,256]{3,2,1,0:T(8,128)} %bitcast.152, ...), custom_call_target="tpu_custom_call", output_to_operand_aliasing={{0}: (9, {})} | custom-call | flops 1 | bytes 1 | tf_op jit(solution)/shard_map/text_back/pallas_call | solution.py:271
  282.4 4.9 %collective-permute-done.33 = bf16[192,1536]{1,0:T(8,128)(2,1)S(1)} collective-permute-done((bf16[192,1536]{1,0:T(8,128)(2,1)S(1)}, bf16[192,1536]{1,0:T(8,128)(2,1)S(1)}, u32[]{:S(2)}, u32[]{:S(2)}) %collective-permute-start.33) | collective-permute-done | bytes 589856 | tf_op jit(solution)/shard_map/ppermute | solution.py:1097
  287.5 3.2 collective-permute-start.35
  291.4 14.6 %attend_back.1 = (bf16[3,3,64,1024]{3,2,1,0:T(8,128)(2,1)}, f32[3,8,64]{2,1,0:T(8,128)}) custom-call(f32[3,3,64,1024]{3,2,1,0:T(8,128)} %bitcast.140, f32[3,3,64,1]{3,2,1,0:T(8,128)} %copy-done.17, f32[4,16,1024]{2,1,0:T(8,128)} %constant.82.clone.table_ref, f32[3,8,1024]{2,1,0:T(8,128)} %copy-done.33, bf16[3,64,1024]{2,1,0:T(8,128)(2,1)} %bitcast.161, ...), custom_call_target="tpu_custom_call" | custom-call | flops 1 | bytes 1 | tf_op jit(solution)/shard_map/attend_back/pallas_call | solution.py:344
  306.0 2.4 convert_add_fusion.out_sum_ref
  308.4 19.1 %first_back.1 = (bf16[4,560,128]{2,1,0:T(8,128)(2,1)}, bf16[4,560,128]{2,1,0:T(8,128)(2,1)}, bf16[4,192,384]{2,1,0:T(8,128)(2,1)}, bf16[4,192,384]{2,1,0:T(8,128...) custom-call(s32[4]{0:T(128)} %copy-done.37, f32[3]{0:T(128)} %copy-done.39, ...), custom_call_target="tpu_custom_call" | custom-call | flops 1 | bytes 1 | tf_op jit(solution)/shard_map/first_back/pallas_call | solution.py:948
  327.6 2.2 collective-permute-done.36
  331.0 3.2 collective-permute-start.39
  334.2 2.9 collective-permute-start.40
  343.2 6.4 %all-to-all-start.2 = ((bf16[16,40,128]{2,1,0:T(8,128)(2,1)}), bf16[16,40,128]{2,1,0:T(8,128)(2,1)S(1)}, u32[]{:S(2)}, u32[]{:S(2)}) async-start(bf16[16,40,128]{2,1,0:T(8,128)(2,1)} %pad_maximum_fusion.13), calls=%async_computation.2 | async-start | bytes 327680 | tf_op jit(solution)/shard_map/all_to_all | solution.py:1124
  349.6 7.0 %collective-permute-done.40 = bf16[4,192,384]{2,1,0:T(8,128)(2,1)S(1)} collective-permute-done((bf16[4,192,384]{2,1,0:T(8,128)(2,1)}, bf16[4,192,384]{2,1,0:T(8,128)(2,1)S(1)}, u32[]{:S(2)}, u32[]{:S(2)}) %collective-permute-start.40) | collective-permute-done | bytes 589856 | tf_op jit(solution)/shard_map/ppermute | solution.py:1115
  357.8 12.5 %all_to_all.33 = bf16[16,32,128]{2,1,0:T(8,128)(2,1)S(1)} all-to-all(bf16[16,32,128]{2,1,0:T(8,128)(2,1)S(1)} %broadcast_in_dim.10), channel_id=1, replica_groups=mesh['row'=8,'col'=16] {'col'}, dimensions={0} | all-to-all | bytes 262144 | tf_op jit(solution)/shard_map/all_to_all | solution.py:96
  373.6 4.0 all-to-all-start.4
  379.2 6.3 %collective-permute-done.42 = bf16[4,192,384]{2,1,0:T(8,128)(2,1)} collective-permute-done((bf16[4,192,384]{2,1,0:T(8,128)(2,1)}, bf16[4,192,384]{2,1,0:T(8,128)(2,1)}, u32[]{:S(2)}, u32[]{:S(2)}) %collective-permute-start.42) | collective-permute-done | bytes 589856 | tf_op jit(solution)/shard_map/ppermute | solution.py:1131
  391.0 2.6 all-to-all-done.4
  (262 shorter events, 85.0 us)
Async XLA Ops:
  9.1 12.8 %collective-permute-start.2 = (bf16[192,384]{1,0:T(8,128)(2,1)S(1)}, bf16[192,384]{1,0:T(8,128)(2,1)S(1)}, u32[]{:S(2)}, u32[]{:S(2)}) collective-permute-start(bf16[192,384]{1,0:T(8,128)(2,1)S(1)} %maximum_maximum_fusion), channel_id=1, source_target_pairs={{12,0},{13,1},{14,2},{15,3},{0,4},{1,5},{2,6},{3,7},{4,8},{5,9},{6... | collective-permute-start | bytes 442376 | tf_op jit(solution)/shard_map/ppermute | solution.py:79
  10.9 25.0 %collective-permute-start.1 = (bf16[192,384]{1,0:T(8,128)(2,1)S(1)}, bf16[192,384]{1,0:T(8,128)(2,1)S(1)}, u32[]{:S(2)}, u32[]{:S(2)}) collective-permute-start(bf16[192,384]{1,0:T(8,128)(2,1)S(1)} %maximum_maximum_fusion), channel_id=1, source_target_pairs={{8,0},{9,1},{10,2},{11,3},{12,4},{13,5},{14,6},{15,7},{0,8},{1,9},... | collective-permute-start | bytes 442376 | tf_op jit(solution)/shard_map/ppermute | solution.py:79
  13.8 22.1 %collective-permute-start = (bf16[192,384]{1,0:T(8,128)(2,1)S(1)}, bf16[192,384]{1,0:T(8,128)(2,1)S(1)}, u32[]{:S(2)}, u32[]{:S(2)}) collective-permute-start(bf16[192,384]{1,0:T(8,128)(2,1)S(1)} %maximum_maximum_fusion), channel_id=1, source_target_pairs={{4,0},{5,1},{6,2},{7,3},{8,4},{9,5},{10,6},{11,7},{12,8},{13,9},{1... | collective-permute-start | bytes 442376 | tf_op jit(solution)/shard_map/ppermute | solution.py:79
  16.4 19.5 %collective-permute-start.5 = (bf16[256,384]{1,0:T(8,128)(2,1)S(1)}, bf16[256,384]{1,0:T(8,128)(2,1)S(1)}, u32[]{:S(2)}, u32[]{:S(2)}) collective-permute-start(bf16[256,384]{1,0:T(8,128)(2,1)S(1)} %pad_maximum_fusion.12), channel_id=1, source_target_pairs={{3,0},{0,1},{1,2},{2,3},{7,4},{4,5},{5,6},{6,7},{11,8},{8,9},{9,10... | collective-permute-start | bytes 589832 | tf_op jit(solution)/shard_map/ppermute | solution.py:79
  18.4 17.5 %collective-permute-start.4 = (bf16[256,384]{1,0:T(8,128)(2,1)S(1)}, bf16[256,384]{1,0:T(8,128)(2,1)S(1)}, u32[]{:S(2)}, u32[]{:S(2)}) collective-permute-start(bf16[256,384]{1,0:T(8,128)(2,1)S(1)} %pad_maximum_fusion.12), channel_id=1, source_target_pairs={{2,0},{3,1},{0,2},{1,3},{6,4},{7,5},{4,6},{5,7},{10,8},{11,9},{8,1... | collective-permute-start | bytes 589832 | tf_op jit(solution)/shard_map/ppermute | solution.py:79
  22.0 13.9 %collective-permute-start.3 = (bf16[256,384]{1,0:T(8,128)(2,1)S(1)}, bf16[256,384]{1,0:T(8,128)(2,1)S(1)}, u32[]{:S(2)}, u32[]{:S(2)}) collective-permute-start(bf16[256,384]{1,0:T(8,128)(2,1)S(1)} %pad_maximum_fusion.12), channel_id=1, source_target_pairs={{1,0},{2,1},{3,2},{0,3},{5,4},{6,5},{7,6},{4,7},{9,8},{10,9},{11,1... | collective-permute-start | bytes 589832 | tf_op jit(solution)/shard_map/ppermute | solution.py:79
  37.5 29.6 %collective-permute-start.7 = (bf16[4,256,384]{2,1,0:T(8,128)(2,1)}, bf16[4,256,384]{2,1,0:T(8,128)(2,1)}, u32[]{:S(2)}, u32[]{:S(2)}) collective-permute-start(bf16[4,256,384]{2,1,0:T(8,128)(2,1)} %pad_maximum_fusion.3.p0_ref), channel_id=1, source_target_pairs={{12,0},{13,1},{14,2},{15,3},{0,4},{1,5},{2,6},{3,7},{4,8},{5,9},{6... | collective-permute-start | bytes 2359304 | tf_op jit(solution)/shard_map/ppermute | solution.py:1023
  38.1 29.1 %collective-permute-start.6 = (bf16[4,256,384]{2,1,0:T(8,128)(2,1)}, bf16[4,256,384]{2,1,0:T(8,128)(2,1)}, u32[]{:S(2)}, u32[]{:S(2)}) collective-permute-start(bf16[4,256,384]{2,1,0:T(8,128)(2,1)} %pad_maximum_fusion.3.p0_ref), channel_id=1, source_target_pairs={{4,0},{5,1},{6,2},{7,3},{8,4},{9,5},{10,6},{11,7},{12,8},{13,9},{1... | collective-permute-start | bytes 2359304 | tf_op jit(solution)/shard_map/ppermute | solution.py:1023
  41.8 24.8 %collective-permute-start.10 = (bf16[4,192,384]{2,1,0:T(8,128)(2,1)S(1)}, bf16[4,192,384]{2,1,0:T(8,128)(2,1)}, u32[]{:S(2)}, u32[]{:S(2)}) collective-permute-start(bf16[4,192,384]{2,1,0:T(8,128)(2,1)S(1)} %pad_maximum_fusion.4.refs_0_), channel_id=1, source_target_pairs={{3,0},{0,1},{1,2},{2,3},{7,4},{4,5},{5,6},{6,7},{11,8},{8,9},{9,10... | collective-permute-start | bytes 1769480 | tf_op jit(solution)/shard_map/ppermute | solution.py:79
  42.4 24.1 %collective-permute-start.9 = (bf16[4,192,384]{2,1,0:T(8,128)(2,1)S(1)}, bf16[4,192,384]{2,1,0:T(8,128)(2,1)}, u32[]{:S(2)}, u32[]{:S(2)}) collective-permute-start(bf16[4,192,384]{2,1,0:T(8,128)(2,1)S(1)} %pad_maximum_fusion.4.refs_0_), channel_id=1, source_target_pairs={{2,0},{3,1},{0,2},{1,3},{6,4},{7,5},{4,6},{5,7},{10,8},{11,9},{8,1... | collective-permute-start | bytes 1769480 | tf_op jit(solution)/shard_map/ppermute | solution.py:79
  44.5 22.7 %collective-permute-start.8 = (bf16[4,192,384]{2,1,0:T(8,128)(2,1)S(1)}, bf16[4,192,384]{2,1,0:T(8,128)(2,1)}, u32[]{:S(2)}, u32[]{:S(2)}) collective-permute-start(bf16[4,192,384]{2,1,0:T(8,128)(2,1)S(1)} %pad_maximum_fusion.4.refs_0_), channel_id=1, source_target_pairs={{1,0},{2,1},{3,2},{0,3},{5,4},{6,5},{7,6},{4,7},{9,8},{10,9},{11,1... | collective-permute-start | bytes 1769480 | tf_op jit(solution)/shard_map/ppermute | solution.py:79
  46.4 10.1 %all-to-all-start.1 = ((bf16[8,16,384]{2,1,0:T(8,128)(2,1)}), bf16[8,16,384]{2,1,0:T(8,128)(2,1)S(1)}, u32[]{:S(2)}, u32[]{:S(2)}) async-start(bf16[8,16,384]{2,1,0:T(8,128)(2,1)} %broadcast_in_dim.9), calls=%async_computation.1 | async-start | bytes 196608 | tf_op jit(solution)/shard_map/all_to_all | solution.py:96
  50.7 83.9 %all-gather.2.cloned.1.call-start = ((), (), s32[]{:S(2)}) async-start(), calls=%async_computation.6 | async-start | bytes 5013504 | tf_op jit(solution)/shard_map/all_gather | solution.py:1028
  67.2 330.6 %reduce-scatter.2.cloned.1.call-start = ((), (), s32[]{:S(2)}) async-start(), calls=%async_computation.7 | async-start | bytes 8355840 | tf_op jit(solution)/shard_map/reduce_scatter | solution.py:1151
  68.6 24.9 %collective-permute-start.11 = (bf16[4,256,384]{2,1,0:T(8,128)(2,1)}, bf16[4,256,384]{2,1,0:T(8,128)(2,1)S(1)}, u32[]{:S(2)}, u32[]{:S(2)}) collective-permute-start(bf16[4,256,384]{2,1,0:T(8,128)(2,1)} %pad_maximum_fusion.3.p0_ref), channel_id=1, source_target_pairs={{8,0},{9,1},{10,2},{11,3},{12,4},{13,5},{14,6},{15,7},{0,8},{1,9},... | collective-permute-start | bytes 2359304 | tf_op jit(solution)/shard_map/ppermute | solution.py:1029
  72.7 38.5 %collective-permute-start.17 = (bf16[192,1536]{1,0:T(8,128)(2,1)S(1)}, bf16[192,1536]{1,0:T(8,128)(2,1)S(1)}, u32[]{:S(2)}, u32[]{:S(2)}) collective-permute-start(bf16[192,1536]{1,0:T(8,128)(2,1)S(1)} %get-tuple-element.145), channel_id=1, source_target_pairs={{96,0},{112,16},{0,32},{16,48},{32,64},{48,80},{64,96},{80,112},{9... | collective-permute-start | bytes 1769480 | tf_op jit(solution)/shard_map/ppermute | solution.py:49
  74.2 38.3 %collective-permute-start.16 = (bf16[192,1536]{1,0:T(8,128)(2,1)S(1)}, bf16[192,1536]{1,0:T(8,128)(2,1)S(1)}, u32[]{:S(2)}, u32[]{:S(2)}) collective-permute-start(bf16[192,1536]{1,0:T(8,128)(2,1)S(1)} %get-tuple-element.145), channel_id=1, source_target_pairs={{64,0},{80,16},{96,32},{112,48},{0,64},{16,80},{32,96},{48,112},{6... | collective-permute-start | bytes 1769480 | tf_op jit(solution)/shard_map/ppermute | solution.py:49
  77.1 35.5 %collective-permute-start.15 = (bf16[192,1536]{1,0:T(8,128)(2,1)S(1)}, bf16[192,1536]{1,0:T(8,128)(2,1)S(1)}, u32[]{:S(2)}, u32[]{:S(2)}) collective-permute-start(bf16[192,1536]{1,0:T(8,128)(2,1)S(1)} %get-tuple-element.145), channel_id=1, source_target_pairs={{32,0},{48,16},{64,32},{80,48},{96,64},{112,80},{0,96},{16,112},{3... | collective-permute-start | bytes 1769480 | tf_op jit(solution)/shard_map/ppermute | solution.py:49
  106.9 12.1 %collective-permute-start.14 = (bf16[192,1024]{1,0:T(8,128)(2,1)S(1)}, bf16[192,1024]{1,0:T(8,128)(2,1)S(1)}, u32[]{:S(2)}, u32[]{:S(2)}) collective-permute-start(bf16[192,1024]{1,0:T(8,128)(2,1)S(1)} %get-tuple-element.141), channel_id=1, source_target_pairs={{96,0},{112,16},{0,32},{16,48},{32,64},{48,80},{64,96},{80,112},{9... | collective-permute-start | bytes 1179656 | tf_op jit(solution)/shard_map/ppermute | solution.py:49
  108.4 17.9 %collective-permute-start.13 = (bf16[192,1024]{1,0:T(8,128)(2,1)S(1)}, bf16[192,1024]{1,0:T(8,128)(2,1)S(1)}, u32[]{:S(2)}, u32[]{:S(2)}) collective-permute-start(bf16[192,1024]{1,0:T(8,128)(2,1)S(1)} %get-tuple-element.141), channel_id=1, source_target_pairs={{64,0},{80,16},{96,32},{112,48},{0,64},{16,80},{32,96},{48,112},{6... | collective-permute-start | bytes 1179656 | tf_op jit(solution)/shard_map/ppermute | solution.py:49
  111.1 15.2 %collective-permute-start.12 = (bf16[192,1024]{1,0:T(8,128)(2,1)S(1)}, bf16[192,1024]{1,0:T(8,128)(2,1)S(1)}, u32[]{:S(2)}, u32[]{:S(2)}) collective-permute-start(bf16[192,1024]{1,0:T(8,128)(2,1)S(1)} %get-tuple-element.141), channel_id=1, source_target_pairs={{32,0},{48,16},{64,32},{80,48},{96,64},{112,80},{0,96},{16,112},{3... | collective-permute-start | bytes 1179656 | tf_op jit(solution)/shard_map/ppermute | solution.py:49
  126.6 8.0 %collective-permute-start.19 = (bf16[4,192,1536]{2,1,0:T(8,128)(2,1)S(1)}, bf16[4,192,1536]{2,1,0:T(8,128)(2,1)}, u32[]{:S(2)}, u32[]{:S(2)}) collective-permute-start(bf16[4,192,1536]{2,1,0:T(8,128)(2,1)S(1)} %pad_maximum_fusion.out_near_ref), channel_id=1, source_target_pairs={{16,0},{0,16},{48,32},{32,48},{80,64},{64,80},{112,96},{96,112},{1... | collective-permute-start | bytes 7077896 | tf_op jit(solution)/shard_map/ppermute | solution.py:54
  128.0 5.5 %collective-permute-start.18 = (bf16[4,192,1024]{2,1,0:T(8,128)(2,1)S(1)}, bf16[4,192,1024]{2,1,0:T(8,128)(2,1)S(1)}, u32[]{:S(2)}, u32[]{:S(2)}) collective-permute-start(bf16[4,192,1024]{2,1,0:T(8,128)(2,1)S(1)} %pad_maximum_fusion.1.near_ref), channel_id=1, source_target_pairs={{16,0},{0,16},{48,32},{32,48},{80,64},{64,80},{112,96},{96,112},{1... | collective-permute-start | bytes 4718600 | tf_op jit(solution)/shard_map/ppermute | solution.py:54
  153.9 3.7 collective-permute-start.20
  160.5 19.7 %collective-permute-start.23 = (bf16[128,1536]{1,0:T(8,128)(2,1)}, bf16[128,1536]{1,0:T(8,128)(2,1)}, u32[]{:S(2)}, u32[]{:S(2)}) collective-permute-start(bf16[128,1536]{1,0:T(8,128)(2,1)} %get-tuple-element.284), channel_id=1, source_target_pairs={{0,96},{16,112},{32,0},{48,16},{64,32},{80,48},{96,64},{112,80},{1... | collective-permute-start | bytes 1179656 | tf_op jit(solution)/shard_map/ppermute | solution.py:67
  162.7 17.5 %collective-permute-start.22 = (bf16[128,1536]{1,0:T(8,128)(2,1)}, bf16[128,1536]{1,0:T(8,128)(2,1)}, u32[]{:S(2)}, u32[]{:S(2)}) collective-permute-start(bf16[128,1536]{1,0:T(8,128)(2,1)} %get-tuple-element.285), channel_id=1, source_target_pairs={{0,64},{16,80},{32,96},{48,112},{64,0},{80,16},{96,32},{112,48},{1... | collective-permute-start | bytes 1179656 | tf_op jit(solution)/shard_map/ppermute | solution.py:67
  163.9 19.9 %collective-permute-start.21 = (bf16[128,1536]{1,0:T(8,128)(2,1)}, bf16[128,1536]{1,0:T(8,128)(2,1)}, u32[]{:S(2)}, u32[]{:S(2)}) collective-permute-start(bf16[128,1536]{1,0:T(8,128)(2,1)} %get-tuple-element.286), channel_id=1, source_target_pairs={{0,32},{16,48},{32,64},{48,80},{64,96},{80,112},{96,0},{112,16},{1... | collective-permute-start | bytes 1179656 | tf_op jit(solution)/shard_map/ppermute | solution.py:67
  186.8 21.3 %collective-permute-start.26 = (bf16[128,1536]{1,0:T(8,128)(2,1)}, bf16[128,1536]{1,0:T(8,128)(2,1)S(1)}, u32[]{:S(2)}, u32[]{:S(2)}) collective-permute-start(bf16[128,1536]{1,0:T(8,128)(2,1)} %get-tuple-element.157), channel_id=1, source_target_pairs={{96,0},{112,16},{0,32},{16,48},{32,64},{48,80},{64,96},{80,112},{9... | collective-permute-start | bytes 1179656 | tf_op jit(solution)/shard_map/ppermute | solution.py:49
  187.2 20.9 %collective-permute-start.25 = (bf16[128,1536]{1,0:T(8,128)(2,1)}, bf16[128,1536]{1,0:T(8,128)(2,1)S(1)}, u32[]{:S(2)}, u32[]{:S(2)}) collective-permute-start(bf16[128,1536]{1,0:T(8,128)(2,1)} %get-tuple-element.157), channel_id=1, source_target_pairs={{64,0},{80,16},{96,32},{112,48},{0,64},{16,80},{32,96},{48,112},{6... | collective-permute-start | bytes 1179656 | tf_op jit(solution)/shard_map/ppermute | solution.py:49
  189.2 19.4 %collective-permute-start.24 = (bf16[128,1536]{1,0:T(8,128)(2,1)}, bf16[128,1536]{1,0:T(8,128)(2,1)S(1)}, u32[]{:S(2)}, u32[]{:S(2)}) collective-permute-start(bf16[128,1536]{1,0:T(8,128)(2,1)} %get-tuple-element.157), channel_id=1, source_target_pairs={{32,0},{48,16},{64,32},{80,48},{96,64},{112,80},{0,96},{16,112},{3... | collective-permute-start | bytes 1179656 | tf_op jit(solution)/shard_map/ppermute | solution.py:49
  241.8 19.8 %collective-permute-start.31 = (bf16[192,1024]{1,0:T(8,128)(2,1)S(1)}, bf16[192,1024]{1,0:T(8,128)(2,1)S(1)}, u32[]{:S(2)}, u32[]{:S(2)}) collective-permute-start(bf16[192,1024]{1,0:T(8,128)(2,1)S(1)} %get-tuple-element.280), channel_id=1, source_target_pairs={{0,96},{16,112},{32,0},{48,16},{64,32},{80,48},{96,64},{112,80},{1... | collective-permute-start | bytes 1179656 | tf_op jit(solution)/shard_map/ppermute | solution.py:67
  244.5 17.1 %collective-permute-start.30 = (bf16[192,1024]{1,0:T(8,128)(2,1)S(1)}, bf16[192,1024]{1,0:T(8,128)(2,1)S(1)}, u32[]{:S(2)}, u32[]{:S(2)}) collective-permute-start(bf16[192,1024]{1,0:T(8,128)(2,1)S(1)} %get-tuple-element.281), channel_id=1, source_target_pairs={{0,64},{16,80},{32,96},{48,112},{64,0},{80,16},{96,32},{112,48},{1... | collective-permute-start | bytes 1179656 | tf_op jit(solution)/shard_map/ppermute | solution.py:67
  244.5 20.5 %collective-permute-start.29 = (bf16[192,1024]{1,0:T(8,128)(2,1)S(1)}, bf16[192,1024]{1,0:T(8,128)(2,1)S(1)}, u32[]{:S(2)}, u32[]{:S(2)}) collective-permute-start(bf16[192,1024]{1,0:T(8,128)(2,1)S(1)} %get-tuple-element.282), channel_id=1, source_target_pairs={{0,32},{16,48},{32,64},{48,80},{64,96},{80,112},{96,0},{112,16},{1... | collective-permute-start | bytes 1179656 | tf_op jit(solution)/shard_map/ppermute | solution.py:67
  265.0 4.5 %collective-permute-start.32 = (bf16[4,192,1536]{2,1,0:T(8,128)(2,1)S(1)}, bf16[4,192,1536]{2,1,0:T(8,128)(2,1)S(1)}, u32[]{:S(2)}, u32[]{:S(2)}) collective-permute-start(bf16[4,192,1536]{2,1,0:T(8,128)(2,1)S(1)} %get-tuple-element.179), channel_id=1, source_target_pairs={{16,0},{0,16},{48,32},{32,48},{80,64},{64,80},{112,96},{96,112},{1... | collective-permute-start | bytes 7077896 | tf_op jit(solution)/shard_map/ppermute | solution.py:62
  270.2 17.1 %collective-permute-start.33 = (bf16[192,1536]{1,0:T(8,128)(2,1)S(1)}, bf16[192,1536]{1,0:T(8,128)(2,1)S(1)}, u32[]{:S(2)}, u32[]{:S(2)}) collective-permute-start(bf16[192,1536]{1,0:T(8,128)(2,1)S(1)} %get-tuple-element.277), channel_id=1, source_target_pairs={{0,64},{16,80},{32,96},{48,112},{64,0},{80,16},{96,32},{112,48},{1... | collective-permute-start | bytes 1769480 | tf_op jit(solution)/shard_map/ppermute | solution.py:1097
  287.4 18.6 %collective-permute-start.34 = (bf16[192,1536]{1,0:T(8,128)(2,1)S(1)}, bf16[192,1536]{1,0:T(8,128)(2,1)S(1)}, u32[]{:S(2)}, u32[]{:S(2)}) collective-permute-start(bf16[192,1536]{1,0:T(8,128)(2,1)S(1)} %get-tuple-element.187), channel_id=1, source_target_pairs={{0,32},{16,48},{32,64},{48,80},{64,96},{80,112},{96,0},{112,16},{1... | collective-permute-start | bytes 1769480 | tf_op jit(solution)/shard_map/ppermute | solution.py:1107
  287.5 18.5 %collective-permute-start.35 = (bf16[192,1536]{1,0:T(8,128)(2,1)S(1)}, bf16[192,1536]{1,0:T(8,128)(2,1)}, u32[]{:S(2)}, u32[]{:S(2)}) collective-permute-start(bf16[192,1536]{1,0:T(8,128)(2,1)S(1)} %get-tuple-element.188), channel_id=1, source_target_pairs={{0,96},{16,112},{32,0},{48,16},{64,32},{80,48},{96,64},{112,80},{1... | collective-permute-start | bytes 1769480 | tf_op jit(solution)/shard_map/ppermute | solution.py:1107
  330.9 8.3 %collective-permute-start.37 = (bf16[560,128]{1,0:T(8,128)(2,1)S(1)}, bf16[560,128]{1,0:T(8,128)(2,1)S(1)}, u32[]{:S(2)}, u32[]{:S(2)}) collective-permute-start(bf16[560,128]{1,0:T(8,128)(2,1)S(1)} %get-tuple-element.288), channel_id=1, source_target_pairs={{0,32},{16,48},{32,64},{48,80},{64,96},{80,112},{96,0},{112,16},{1... | collective-permute-start | bytes 430088 | tf_op jit(solution)/shard_map/ppermute | solution.py:67
  331.0 9.4 %collective-permute-start.39 = (bf16[560,128]{1,0:T(8,128)(2,1)S(1)}, bf16[560,128]{1,0:T(8,128)(2,1)S(1)}, u32[]{:S(2)}, u32[]{:S(2)}) collective-permute-start(bf16[560,128]{1,0:T(8,128)(2,1)S(1)} %get-tuple-element.289), channel_id=1, source_target_pairs={{0,96},{16,112},{32,0},{48,16},{64,32},{80,48},{96,64},{112,80},{1... | collective-permute-start | bytes 430088 | tf_op jit(solution)/shard_map/ppermute | solution.py:67
  334.2 6.9 %collective-permute-start.38 = (bf16[560,128]{1,0:T(8,128)(2,1)S(1)}, bf16[560,128]{1,0:T(8,128)(2,1)S(1)}, u32[]{:S(2)}, u32[]{:S(2)}) collective-permute-start(bf16[560,128]{1,0:T(8,128)(2,1)S(1)} %get-tuple-element.290), channel_id=1, source_target_pairs={{0,64},{16,80},{32,96},{48,112},{64,0},{80,16},{96,32},{112,48},{1... | collective-permute-start | bytes 430088 | tf_op jit(solution)/shard_map/ppermute | solution.py:67
  334.2 22.4 %collective-permute-start.40 = (bf16[4,192,384]{2,1,0:T(8,128)(2,1)}, bf16[4,192,384]{2,1,0:T(8,128)(2,1)S(1)}, u32[]{:S(2)}, u32[]{:S(2)}) collective-permute-start(bf16[4,192,384]{2,1,0:T(8,128)(2,1)} %get-tuple-element.203), channel_id=1, source_target_pairs={{0,1},{1,2},{2,3},{3,0},{4,5},{5,6},{6,7},{7,4},{8,9},{9,10},{10,1... | collective-permute-start | bytes 1769480 | tf_op jit(solution)/shard_map/ppermute | solution.py:1115
  337.1 19.5 %collective-permute-start.41 = (bf16[4,192,384]{2,1,0:T(8,128)(2,1)}, bf16[4,192,384]{2,1,0:T(8,128)(2,1)S(1)}, u32[]{:S(2)}, u32[]{:S(2)}) collective-permute-start(bf16[4,192,384]{2,1,0:T(8,128)(2,1)} %get-tuple-element.204), channel_id=1, source_target_pairs={{0,3},{1,0},{2,1},{3,2},{4,7},{5,4},{6,5},{7,6},{8,11},{9,8},{10,9... | collective-permute-start | bytes 1769480 | tf_op jit(solution)/shard_map/ppermute | solution.py:1115
  343.2 14.5 %all-to-all-start.2 = ((bf16[16,40,128]{2,1,0:T(8,128)(2,1)}), bf16[16,40,128]{2,1,0:T(8,128)(2,1)S(1)}, u32[]{:S(2)}, u32[]{:S(2)}) async-start(bf16[16,40,128]{2,1,0:T(8,128)(2,1)} %pad_maximum_fusion.13), calls=%async_computation.2 | async-start | bytes 327680 | tf_op jit(solution)/shard_map/all_to_all | solution.py:1124
  370.3 15.3 %collective-permute-start.42 = (bf16[4,192,384]{2,1,0:T(8,128)(2,1)}, bf16[4,192,384]{2,1,0:T(8,128)(2,1)}, u32[]{:S(2)}, u32[]{:S(2)}) collective-permute-start(bf16[4,192,384]{2,1,0:T(8,128)(2,1)} %get-tuple-element.208), channel_id=1, source_target_pairs={{0,2},{1,3},{2,0},{3,1},{4,6},{5,7},{6,4},{7,5},{8,10},{9,11},{10,... | collective-permute-start | bytes 1769480 | tf_op jit(solution)/shard_map/ppermute | solution.py:1131
  373.6 20.0 %all-to-all-start.4 = ((bf16[8,16,32,128]{3,2,1,0:T(8,128)(2,1)}), bf16[8,16,32,128]{3,2,1,0:T(8,128)(2,1)S(1)}, u32[]{:S(2)}, u32[]{:S(2)}) async-start(bf16[8,16,32,128]{3,2,1,0:T(8,128)(2,1)} %broadcast_in_dim.11), calls=%async_computation.4 | async-start | bytes 2097152 | tf_op jit(solution)/shard_map/all_to_all | solution.py:96
  387.7 13.1 %collective-permute-start.45 = (bf16[192,384]{1,0:T(8,128)(2,1)}, bf16[192,384]{1,0:T(8,128)(2,1)}, u32[]{:S(2)}, u32[]{:S(2)}) collective-permute-start(bf16[192,384]{1,0:T(8,128)(2,1)} %get-tuple-element.293), channel_id=1, source_target_pairs={{0,12},{1,13},{2,14},{3,15},{4,0},{5,1},{6,2},{7,3},{8,4},{9,5},{1... | collective-permute-start | bytes 442376 | tf_op jit(solution)/shard_map/ppermute | solution.py:91
  389.4 11.4 %collective-permute-start.44 = (bf16[192,384]{1,0:T(8,128)(2,1)}, bf16[192,384]{1,0:T(8,128)(2,1)}, u32[]{:S(2)}, u32[]{:S(2)}) collective-permute-start(bf16[192,384]{1,0:T(8,128)(2,1)} %get-tuple-element.294), channel_id=1, source_target_pairs={{0,8},{1,9},{2,10},{3,11},{4,12},{5,13},{6,14},{7,15},{8,0},{9,1},... | collective-permute-start | bytes 442376 | tf_op jit(solution)/shard_map/ppermute | solution.py:91
  390.4 10.4 %collective-permute-start.43 = (bf16[192,384]{1,0:T(8,128)(2,1)S(1)}, bf16[192,384]{1,0:T(8,128)(2,1)}, u32[]{:S(2)}, u32[]{:S(2)}) collective-permute-start(bf16[192,384]{1,0:T(8,128)(2,1)S(1)} %get-tuple-element.295), channel_id=1, source_target_pairs={{0,4},{1,5},{2,6},{3,7},{4,8},{5,9},{6,10},{7,11},{8,12},{9,13},{1... | collective-permute-start | bytes 442376 | tf_op jit(solution)/shard_map/ppermute | solution.py:91
  (57 other events, 696.4 us)
Sparse Core Ops, SparseCore 0:
  67.3 55.4 all-gather.1
  287.5 97.0 reduce-scatter.1

commit v2 on v1

--- a/solution.py
+++ b/solution.py
@@ -64,7 +64,7 @@
 
 
 def to_chips(near):
-    return [near[0]] + [lax.ppermute(near[d], "row", row_pairs_to(d, 0)) for d in (1, 2, 3)]
+    return [near[0]] + [lax.ppermute(near[d], "row", row_pairs_to(d, 0)) for d in (1, 3, 2)]
 
 
 def col_pairs_to(dy, dz):
@@ -88,7 +88,7 @@
 
 
 def along_col(parts, step):
-    return [parts[0]] + [lax.ppermute(parts[d], "col", col_pairs_to(*step(d))) for d in (1, 2, 3)]
+    return [parts[0]] + [lax.ppermute(parts[d], "col", col_pairs_to(*step(d))) for d in (1, 3, 2)]
 
 
 def send_all(piece, axis):

time: 420 us -> 417 us (level)
  waiting for transfers between devices: 115 us -> 105 us
  starting transfers between devices: 76.4 us -> 83.2 us
    ppermute x9, waiting for transfers between devices: 24.3 us -> 18.1 us  [to_chips(): lax.ppermute(near[d], 'row', row_pairs_to(d, 0))]
  transfers between devices with their start and end apart: 51 -> 51, of which waited for: 25 -> 26; matrix products, arithmetic and copies ran while one was open for 7% -> 7% of each run, Pallas kernels for 21% -> 21%
where the time goes in v2:
time: 417 us; the launch traced here: 409 us
  Pallas kernels  130 us (31%)
  waiting for transfers between devices  105 us (25%)
  starting transfers between devices  83.2 us (20%)
  local copies, waits for them, and re-layouts  28 us (7%)
  blocking collectives  23.6 us (6%)
  other arithmetic  22.3 us (5%)
  between operations  15.1 us (4%)
    ppermute x9, waiting for transfers between devices, from_chips(): lax.ppermute(piece, 'row', row_pairs(d, 0))  24.1 us
    pallas_call x1, Pallas kernels, backward(): pl.pallas_call(backward_kernel, grid_spec=pltpu.PrefetchScalarGridSpec(nu...  23.6 us
    pallas_call x1, Pallas kernels, forward(): pl.pallas_call(forward_kernel, grid_spec=pltpu.PrefetchScalarGridSpec(num...  19.2 us
    pallas_call x1, Pallas kernels, first_back(): pl.pallas_call(first_kernel, grid_spec=pltpu.PrefetchScalarGridSpec(num_s...  19.1 us
    ppermute x9, waiting for transfers between devices, to_chips(): lax.ppermute(near[d], 'row', row_pairs_to(d, 0))  18.1 us
    ppermute x9, starting transfers between devices, from_chips(): lax.ppermute(piece, 'row', row_pairs(d, 0))  17.2 us
    ppermute x9, starting transfers between devices, from_col(): lax.ppermute(piece, 'col', col_pairs(*step(d)))  16.5 us
    pallas_call x1, Pallas kernels, weight_grads(): pl.pallas_call(weight_kernel, grid=(4,), in_specs=[lane_block(TOKENS, wid...  14.9 us
  transfers between devices with their start and end apart: 51, of which 26 were waited for; matrix products, arithmetic and copies ran while one was open for 7% of the time, Pallas kernels for 21%

profile of v2, /device:TPU:0, one launch (start us, length us, event | category | flops | bytes accessed | tf_op | source)
XLA Modules:
  0.0 408.8 jit_solution(11680625534867072237)
XLA Ops:
  10.9 2.9 collective-permute-start.1
  18.4 3.6 collective-permute-start.4
  24.7 11.1 %all_to_all.32 = bf16[16,2,192]{2,1,0:T(2,128)(2,1)S(1)} all-to-all(bf16[16,2,192]{2,1,0:T(2,128)(2,1)S(1)} %reshape.243), channel_id=1, replica_groups=mesh['row'=8,'col'=16] {'col'}, dimensions={0} | all-to-all | bytes 24576 | tf_op jit(solution)/shard_map/all_to_all | solution.py:1016
  38.1 2.7 collective-permute-start.6
  46.4 4.3 %all-to-all-start.1 = ((bf16[8,16,384]{2,1,0:T(8,128)(2,1)}), bf16[8,16,384]{2,1,0:T(8,128)(2,1)S(1)}, u32[]{:S(2)}, u32[]{:S(2)}) async-start(bf16[8,16,384]{2,1,0:T(8,128)(2,1)} %broadcast_in_dim.9), calls=%async_computation.1 | async-start | bytes 196608 | tf_op jit(solution)/shard_map/all_to_all | solution.py:96
  52.4 4.1 %all-to-all-done.1.packed_ref = bf16[8,16,384]{2,1,0:T(8,128)(2,1)S(1)} async-done(((bf16[8,16,384]{2,1,0:T(8,128)(2,1)}), bf16[8,16,384]{2,1,0:T(8,128)(2,1)S(1)}, u32[]{:S(2)}, u32[]{:S(2)}) %all-to-all-start.1) | async-done | bytes 98336 | tf_op jit(solution)/shard_map/all_to_all | solution.py:96
  58.1 8.5 %collective-permute-done.10.refs_3_ = bf16[4,192,384]{2,1,0:T(8,128)(2,1)} collective-permute-done((bf16[4,192,384]{2,1,0:T(8,128)(2,1)S(1)}, bf16[4,192,384]{2,1,0:T(8,128)(2,1)}, u32[]{:S(2)}, u32[]{:S(2)}) %collective-permute-start.10) | collective-permute-done | bytes 589856 | tf_op jit(solution)/shard_map/ppermute | solution.py:79
  69.6 3.1 unpack_head.1
  74.2 2.8 collective-permute-start.16
  78.7 6.3 %qkv_project.1 = f32[3,192,1024]{2,1,0:T(8,128)S(1)} custom-call(bf16[144,1024]{1,0:T(8,128)(2,1)S(1)} %get-tuple-element.129.patch_ref, bf16[144,1536]{1,0:T(8,128)(2,1)S(1)} %bitcast.143, f32[8,1536]{1,0:T(8,128)S(1)} %select_maximum_fusion.vec_ref, bf16[3,1536,192]{2,1,0:T(8,128)(2,1)S(1)} %get-tuple-element.134.weight_ref), custom_call_target="tpu_custom_call" | custom-call | flops 1 | bytes 1 | tf_op jit(solution)/shard_map/qkv_project/pallas_call | solution.py:512
  85.1 8.4 %collective-permute-done.11.p2_ref = bf16[4,256,384]{2,1,0:T(8,128)(2,1)S(1)} collective-permute-done((bf16[4,256,384]{2,1,0:T(8,128)(2,1)}, bf16[4,256,384]{2,1,0:T(8,128)(2,1)S(1)}, u32[]{:S(2)}, u32[]{:S(2)}) %collective-permute-start.11) | collective-permute-done | bytes 786464 | tf_op jit(solution)/shard_map/ppermute | solution.py:1029
  93.4 3.2 text_project.1
  96.7 10.2 %attend.1 = (bf16[192,1024]{1,0:T(8,128)(2,1)S(1)}, f32[3,8,1024]{2,1,0:T(8,128)S(1)}) custom-call(s32[1]{0:T(128)} %dynamic_slice.14.cap_ref, f32[3]{0:T(128)S(1)} %dynamic-slice_tanh_fusion.gate_ref, f32[3,3,64,1024]{3,2,1,0:T(8,128)S(1)} %bitcast.138, f32[2,3,64,256]{3,2,1,0:T(8,128)S(1)} %bitcast.151, f32[3,3,64,1]{3,2,1,0:T(8,128)S(1)} %reshape.242.gain_ref, ...), custom_call_target="tpu_custom_call" | custom-call | flops 1 | bytes 1 | tf_op jit(solution)/shard_map/attend/pallas_call | solution.py:195
  108.4 2.7 collective-permute-start.13
  112.6 6.4 %collective-permute-done.14 = bf16[192,1024]{1,0:T(8,128)(2,1)S(1)} collective-permute-done((bf16[192,1024]{1,0:T(8,128)(2,1)S(1)}, bf16[192,1024]{1,0:T(8,128)(2,1)S(1)}, u32[]{:S(2)}, u32[]{:S(2)}) %collective-permute-start.14) | collective-permute-done | bytes 393248 | tf_op jit(solution)/shard_map/ppermute | solution.py:49
  119.0 7.3 %collective-permute-done.13 = bf16[192,1024]{1,0:T(8,128)(2,1)S(1)} collective-permute-done((bf16[192,1024]{1,0:T(8,128)(2,1)S(1)}, bf16[192,1024]{1,0:T(8,128)(2,1)S(1)}, u32[]{:S(2)}, u32[]{:S(2)}) %collective-permute-start.13) | collective-permute-done | bytes 393248 | tf_op jit(solution)/shard_map/ppermute | solution.py:49
  129.2 4.3 %collective-permute-done.18.far_ref = bf16[4,192,1024]{2,1,0:T(8,128)(2,1)S(1)} collective-permute-done((bf16[4,192,1024]{2,1,0:T(8,128)(2,1)S(1)}, bf16[4,192,1024]{2,1,0:T(8,128)(2,1)S(1)}, u32[]{:S(2)}, u32[]{:S(2)}) %collective-permute-start.18) | collective-permute-done | bytes 1572896 | tf_op jit(solution)/shard_map/ppermute | solution.py:54
  134.6 19.2 %forward.1 = (bf16[1024,1536]{1,0:T(8,128)(2,1)}, bf16[1024,1536]{1,0:T(8,128)(2,1)}, bf16[1024,1024]{1,0:T(8,128)(2,1)}, bf16[1024,512]{1,0:T(8,128)(2,1)}, bf1...) custom-call(s32[4]{0:T(128)} %copy-done.37, bf16[4,192,1024]{2,1,0:T(8,128)(2,1)} %copy-done.5, ...), custom_call_target="tpu_custom_call" | custom-call | flops 1 | bytes 1 | tf_op jit(solution)/shard_map/forward/pallas_call | solution.py:560
  154.0 3.5 collective-permute-done.20
  157.5 2.9 fusion.7
  160.5 2.7 collective-permute-start.23
  166.6 7.7 %collective-permute-done.23.p3_ref = bf16[128,1536]{1,0:T(8,128)(2,1)} collective-permute-done((bf16[128,1536]{1,0:T(8,128)(2,1)}, bf16[128,1536]{1,0:T(8,128)(2,1)}, u32[]{:S(2)}, u32[]{:S(2)}) %collective-permute-start.23) | collective-permute-done | bytes 393248 | tf_op jit(solution)/shard_map/ppermute | solution.py:67
  174.4 7.1 %collective-permute-done.22.p2_ref = bf16[128,1536]{1,0:T(8,128)(2,1)} collective-permute-done((bf16[128,1536]{1,0:T(8,128)(2,1)}, bf16[128,1536]{1,0:T(8,128)(2,1)}, u32[]{:S(2)}, u32[]{:S(2)}) %collective-permute-start.22) | collective-permute-done | bytes 393248 | tf_op jit(solution)/shard_map/ppermute | solution.py:67
  181.9 2.9 own_grad.1
  186.5 2.4 collective-permute-start.25
  194.2 2.2 own_block.1
  198.3 8.3 %collective-permute-done.25 = bf16[128,1536]{1,0:T(8,128)(2,1)S(1)} collective-permute-done((bf16[128,1536]{1,0:T(8,128)(2,1)}, bf16[128,1536]{1,0:T(8,128)(2,1)S(1)}, u32[]{:S(2)}, u32[]{:S(2)}) %collective-permute-start.25) | collective-permute-done | bytes 393248 | tf_op jit(solution)/shard_map/ppermute | solution.py:49
  207.1 3.4 collective-permute-done.27.other_ref
  210.5 23.6 %backward.1 = (bf16[1024,1536]{1,0:T(8,128)(2,1)S(1)}, bf16[1024,1024]{1,0:T(8,128)(2,1)S(1)}, bf16[1024,1536]{1,0:T(8,128)(2,1)}, bf16[1024,1536]{1,0:T(8,128)(...) custom-call(s32[4]{0:T(128)S(1)} %copy-done.38, ...), custom_call_target="tpu_custom_call" | custom-call | flops 1 | bytes 1 | tf_op jit(solution)/shard_map/backward/pallas_call | solution.py:726
  235.9 3.3 collective-permute-done.28
  239.9 2.7 collective-permute-start.31
  244.6 14.9 %weight_grads.1 = (bf16[16,640,384]{2,1,0:T(8,128)(2,1)}, bf16[4,192,1536]{2,1,0:T(8,128)(2,1)S(1)}, bf16[4,192,1536]{2,1,0:T(8,128)(2,1)S(1)}) custom-call(bf16[1024,1536]{1,0:T(8,128)(2,1)S(1)} %copy-done.20, bf16[1024,1024]{1,0:T(8,128)(2,1)S(1)} %get-tuple-element.166.d_gate_up_ref, bf16[1024,1536]{1,0:T(8,128)(2,1)} %copy-done.21, ...), custom_call_target="tpu_custom_call" | custom-call | flops 1 | bytes 1 | tf_op jit(solution)/shard_map/weight_grads/pallas_call | solution.py:803
  261.1 4.5 %collective-permute-done.32 = bf16[4,192,1536]{2,1,0:T(8,128)(2,1)S(1)} collective-permute-done((bf16[4,192,1536]{2,1,0:T(8,128)(2,1)S(1)}, bf16[4,192,1536]{2,1,0:T(8,128)(2,1)S(1)}, u32[]{:S(2)}, u32[]{:S(2)}) %collective-permute-start.32) | collective-permute-done | bytes 2359328 | tf_op jit(solution)/shard_map/ppermute | solution.py:62
  266.3 2.9 collective-permute-start.33
  270.1 10.3 %text_back.1 = (bf16[16,640,384]{2,1,0:T(8,128)(2,1)}, f32[3,64,1024]{2,1,0:T(8,128)}, f32[3,8,64]{2,1,0:T(8,128)}) custom-call(s32[1]{0:T(128)} %dynamic_slice.14.cap_ref, f32[3]{0:T(128)} %copy-done.39, f32[3,3,64,1024]{3,2,1,0:T(8,128)} %bitcast.139, f32[2,3,64,256]{3,2,1,0:T(8,128)} %bitcast.152, ...), custom_call_target="tpu_custom_call", output_to_operand_aliasing={{0}: (9, {})} | custom-call | flops 1 | bytes 1 | tf_op jit(solution)/shard_map/text_back/pallas_call | solution.py:271
  280.5 2.9 collective-permute-done.33
  287.5 14.6 %attend_back.1 = (bf16[3,3,64,1024]{3,2,1,0:T(8,128)(2,1)}, f32[3,8,64]{2,1,0:T(8,128)}) custom-call(f32[3,3,64,1024]{3,2,1,0:T(8,128)} %bitcast.140, f32[3,3,64,1]{3,2,1,0:T(8,128)} %copy-done.17, f32[4,16,1024]{2,1,0:T(8,128)} %constant.82.clone.table_ref, f32[3,8,1024]{2,1,0:T(8,128)} %copy-done.33, bf16[3,64,1024]{2,1,0:T(8,128)(2,1)} %bitcast.161, ...), custom_call_target="tpu_custom_call" | custom-call | flops 1 | bytes 1 | tf_op jit(solution)/shard_map/attend_back/pallas_call | solution.py:344
  302.1 2.4 convert_add_fusion.out_sum_ref
  304.5 19.1 %first_back.1 = (bf16[4,560,128]{2,1,0:T(8,128)(2,1)}, bf16[4,560,128]{2,1,0:T(8,128)(2,1)}, bf16[4,192,384]{2,1,0:T(8,128)(2,1)}, bf16[4,192,384]{2,1,0:T(8,128...) custom-call(s32[4]{0:T(128)} %copy-done.37, f32[3]{0:T(128)} %copy-done.39, ...), custom_call_target="tpu_custom_call" | custom-call | flops 1 | bytes 1 | tf_op jit(solution)/shard_map/first_back/pallas_call | solution.py:948
  323.6 2.2 collective-permute-done.36
  327.3 2.3 collective-permute-start.39
  330.8 3.4 collective-permute-start.40
  334.2 2.3 collective-permute-start.41
  339.8 6.7 %all-to-all-start.2 = ((bf16[16,40,128]{2,1,0:T(8,128)(2,1)}), bf16[16,40,128]{2,1,0:T(8,128)(2,1)S(1)}, u32[]{:S(2)}, u32[]{:S(2)}) async-start(bf16[16,40,128]{2,1,0:T(8,128)(2,1)} %pad_maximum_fusion.13), calls=%async_computation.2 | async-start | bytes 327680 | tf_op jit(solution)/shard_map/all_to_all | solution.py:1124
  346.5 7.5 %collective-permute-done.40 = bf16[4,192,384]{2,1,0:T(8,128)(2,1)S(1)} collective-permute-done((bf16[4,192,384]{2,1,0:T(8,128)(2,1)}, bf16[4,192,384]{2,1,0:T(8,128)(2,1)S(1)}, u32[]{:S(2)}, u32[]{:S(2)}) %collective-permute-start.40) | collective-permute-done | bytes 589856 | tf_op jit(solution)/shard_map/ppermute | solution.py:1115
  355.0 12.5 %all_to_all.33 = bf16[16,32,128]{2,1,0:T(8,128)(2,1)S(1)} all-to-all(bf16[16,32,128]{2,1,0:T(8,128)(2,1)S(1)} %broadcast_in_dim.10), channel_id=1, replica_groups=mesh['row'=8,'col'=16] {'col'}, dimensions={0} | all-to-all | bytes 262144 | tf_op jit(solution)/shard_map/all_to_all | solution.py:96
  370.9 4.0 all-to-all-start.4
  376.5 7.3 %collective-permute-done.42 = bf16[4,192,384]{2,1,0:T(8,128)(2,1)} collective-permute-done((bf16[4,192,384]{2,1,0:T(8,128)(2,1)}, bf16[4,192,384]{2,1,0:T(8,128)(2,1)}, u32[]{:S(2)}, u32[]{:S(2)}) %collective-permute-start.42) | collective-permute-done | bytes 589856 | tf_op jit(solution)/shard_map/ppermute | solution.py:1131
  (262 shorter events, 90.1 us)
Async XLA Ops:
  9.1 12.8 %collective-permute-start.2 = (bf16[192,384]{1,0:T(8,128)(2,1)S(1)}, bf16[192,384]{1,0:T(8,128)(2,1)S(1)}, u32[]{:S(2)}, u32[]{:S(2)}) collective-permute-start(bf16[192,384]{1,0:T(8,128)(2,1)S(1)} %maximum_maximum_fusion), channel_id=1, source_target_pairs={{12,0},{13,1},{14,2},{15,3},{0,4},{1,5},{2,6},{3,7},{4,8},{5,9},{6... | collective-permute-start | bytes 442376 | tf_op jit(solution)/shard_map/ppermute | solution.py:79
  10.9 25.0 %collective-permute-start.1 = (bf16[192,384]{1,0:T(8,128)(2,1)S(1)}, bf16[192,384]{1,0:T(8,128)(2,1)S(1)}, u32[]{:S(2)}, u32[]{:S(2)}) collective-permute-start(bf16[192,384]{1,0:T(8,128)(2,1)S(1)} %maximum_maximum_fusion), channel_id=1, source_target_pairs={{8,0},{9,1},{10,2},{11,3},{12,4},{13,5},{14,6},{15,7},{0,8},{1,9},... | collective-permute-start | bytes 442376 | tf_op jit(solution)/shard_map/ppermute | solution.py:79
  13.8 22.1 %collective-permute-start = (bf16[192,384]{1,0:T(8,128)(2,1)S(1)}, bf16[192,384]{1,0:T(8,128)(2,1)S(1)}, u32[]{:S(2)}, u32[]{:S(2)}) collective-permute-start(bf16[192,384]{1,0:T(8,128)(2,1)S(1)} %maximum_maximum_fusion), channel_id=1, source_target_pairs={{4,0},{5,1},{6,2},{7,3},{8,4},{9,5},{10,6},{11,7},{12,8},{13,9},{1... | collective-permute-start | bytes 442376 | tf_op jit(solution)/shard_map/ppermute | solution.py:79
  16.4 19.5 %collective-permute-start.5 = (bf16[256,384]{1,0:T(8,128)(2,1)S(1)}, bf16[256,384]{1,0:T(8,128)(2,1)S(1)}, u32[]{:S(2)}, u32[]{:S(2)}) collective-permute-start(bf16[256,384]{1,0:T(8,128)(2,1)S(1)} %pad_maximum_fusion.12), channel_id=1, source_target_pairs={{3,0},{0,1},{1,2},{2,3},{7,4},{4,5},{5,6},{6,7},{11,8},{8,9},{9,10... | collective-permute-start | bytes 589832 | tf_op jit(solution)/shard_map/ppermute | solution.py:79
  18.4 17.5 %collective-permute-start.4 = (bf16[256,384]{1,0:T(8,128)(2,1)S(1)}, bf16[256,384]{1,0:T(8,128)(2,1)S(1)}, u32[]{:S(2)}, u32[]{:S(2)}) collective-permute-start(bf16[256,384]{1,0:T(8,128)(2,1)S(1)} %pad_maximum_fusion.12), channel_id=1, source_target_pairs={{2,0},{3,1},{0,2},{1,3},{6,4},{7,5},{4,6},{5,7},{10,8},{11,9},{8,1... | collective-permute-start | bytes 589832 | tf_op jit(solution)/shard_map/ppermute | solution.py:79
  22.0 13.9 %collective-permute-start.3 = (bf16[256,384]{1,0:T(8,128)(2,1)S(1)}, bf16[256,384]{1,0:T(8,128)(2,1)S(1)}, u32[]{:S(2)}, u32[]{:S(2)}) collective-permute-start(bf16[256,384]{1,0:T(8,128)(2,1)S(1)} %pad_maximum_fusion.12), channel_id=1, source_target_pairs={{1,0},{2,1},{3,2},{0,3},{5,4},{6,5},{7,6},{4,7},{9,8},{10,9},{11,1... | collective-permute-start | bytes 589832 | tf_op jit(solution)/shard_map/ppermute | solution.py:79
  37.5 29.6 %collective-permute-start.7 = (bf16[4,256,384]{2,1,0:T(8,128)(2,1)}, bf16[4,256,384]{2,1,0:T(8,128)(2,1)}, u32[]{:S(2)}, u32[]{:S(2)}) collective-permute-start(bf16[4,256,384]{2,1,0:T(8,128)(2,1)} %pad_maximum_fusion.3.p0_ref), channel_id=1, source_target_pairs={{12,0},{13,1},{14,2},{15,3},{0,4},{1,5},{2,6},{3,7},{4,8},{5,9},{6... | collective-permute-start | bytes 2359304 | tf_op jit(solution)/shard_map/ppermute | solution.py:1023
  38.1 29.1 %collective-permute-start.6 = (bf16[4,256,384]{2,1,0:T(8,128)(2,1)}, bf16[4,256,384]{2,1,0:T(8,128)(2,1)}, u32[]{:S(2)}, u32[]{:S(2)}) collective-permute-start(bf16[4,256,384]{2,1,0:T(8,128)(2,1)} %pad_maximum_fusion.3.p0_ref), channel_id=1, source_target_pairs={{4,0},{5,1},{6,2},{7,3},{8,4},{9,5},{10,6},{11,7},{12,8},{13,9},{1... | collective-permute-start | bytes 2359304 | tf_op jit(solution)/shard_map/ppermute | solution.py:1023
  41.8 24.8 %collective-permute-start.10 = (bf16[4,192,384]{2,1,0:T(8,128)(2,1)S(1)}, bf16[4,192,384]{2,1,0:T(8,128)(2,1)}, u32[]{:S(2)}, u32[]{:S(2)}) collective-permute-start(bf16[4,192,384]{2,1,0:T(8,128)(2,1)S(1)} %pad_maximum_fusion.4.refs_0_), channel_id=1, source_target_pairs={{3,0},{0,1},{1,2},{2,3},{7,4},{4,5},{5,6},{6,7},{11,8},{8,9},{9,10... | collective-permute-start | bytes 1769480 | tf_op jit(solution)/shard_map/ppermute | solution.py:79
  42.4 24.1 %collective-permute-start.9 = (bf16[4,192,384]{2,1,0:T(8,128)(2,1)S(1)}, bf16[4,192,384]{2,1,0:T(8,128)(2,1)}, u32[]{:S(2)}, u32[]{:S(2)}) collective-permute-start(bf16[4,192,384]{2,1,0:T(8,128)(2,1)S(1)} %pad_maximum_fusion.4.refs_0_), channel_id=1, source_target_pairs={{2,0},{3,1},{0,2},{1,3},{6,4},{7,5},{4,6},{5,7},{10,8},{11,9},{8,1... | collective-permute-start | bytes 1769480 | tf_op jit(solution)/shard_map/ppermute | solution.py:79
  44.5 22.7 %collective-permute-start.8 = (bf16[4,192,384]{2,1,0:T(8,128)(2,1)S(1)}, bf16[4,192,384]{2,1,0:T(8,128)(2,1)}, u32[]{:S(2)}, u32[]{:S(2)}) collective-permute-start(bf16[4,192,384]{2,1,0:T(8,128)(2,1)S(1)} %pad_maximum_fusion.4.refs_0_), channel_id=1, source_target_pairs={{1,0},{2,1},{3,2},{0,3},{5,4},{6,5},{7,6},{4,7},{9,8},{10,9},{11,1... | collective-permute-start | bytes 1769480 | tf_op jit(solution)/shard_map/ppermute | solution.py:79
  46.4 10.1 %all-to-all-start.1 = ((bf16[8,16,384]{2,1,0:T(8,128)(2,1)}), bf16[8,16,384]{2,1,0:T(8,128)(2,1)S(1)}, u32[]{:S(2)}, u32[]{:S(2)}) async-start(bf16[8,16,384]{2,1,0:T(8,128)(2,1)} %broadcast_in_dim.9), calls=%async_computation.1 | async-start | bytes 196608 | tf_op jit(solution)/shard_map/all_to_all | solution.py:96
  50.7 83.9 %all-gather.2.cloned.1.call-start = ((), (), s32[]{:S(2)}) async-start(), calls=%async_computation.6 | async-start | bytes 5013504 | tf_op jit(solution)/shard_map/all_gather | solution.py:1028
  67.2 327.8 %reduce-scatter.2.cloned.1.call-start = ((), (), s32[]{:S(2)}) async-start(), calls=%async_computation.7 | async-start | bytes 8355840 | tf_op jit(solution)/shard_map/reduce_scatter | solution.py:1151
  68.6 24.9 %collective-permute-start.11 = (bf16[4,256,384]{2,1,0:T(8,128)(2,1)}, bf16[4,256,384]{2,1,0:T(8,128)(2,1)S(1)}, u32[]{:S(2)}, u32[]{:S(2)}) collective-permute-start(bf16[4,256,384]{2,1,0:T(8,128)(2,1)} %pad_maximum_fusion.3.p0_ref), channel_id=1, source_target_pairs={{8,0},{9,1},{10,2},{11,3},{12,4},{13,5},{14,6},{15,7},{0,8},{1,9},... | collective-permute-start | bytes 2359304 | tf_op jit(solution)/shard_map/ppermute | solution.py:1029
  72.7 38.5 %collective-permute-start.17 = (bf16[192,1536]{1,0:T(8,128)(2,1)S(1)}, bf16[192,1536]{1,0:T(8,128)(2,1)S(1)}, u32[]{:S(2)}, u32[]{:S(2)}) collective-permute-start(bf16[192,1536]{1,0:T(8,128)(2,1)S(1)} %get-tuple-element.145), channel_id=1, source_target_pairs={{96,0},{112,16},{0,32},{16,48},{32,64},{48,80},{64,96},{80,112},{9... | collective-permute-start | bytes 1769480 | tf_op jit(solution)/shard_map/ppermute | solution.py:49
  74.2 38.3 %collective-permute-start.16 = (bf16[192,1536]{1,0:T(8,128)(2,1)S(1)}, bf16[192,1536]{1,0:T(8,128)(2,1)S(1)}, u32[]{:S(2)}, u32[]{:S(2)}) collective-permute-start(bf16[192,1536]{1,0:T(8,128)(2,1)S(1)} %get-tuple-element.145), channel_id=1, source_target_pairs={{64,0},{80,16},{96,32},{112,48},{0,64},{16,80},{32,96},{48,112},{6... | collective-permute-start | bytes 1769480 | tf_op jit(solution)/shard_map/ppermute | solution.py:49
  77.1 35.5 %collective-permute-start.15 = (bf16[192,1536]{1,0:T(8,128)(2,1)S(1)}, bf16[192,1536]{1,0:T(8,128)(2,1)S(1)}, u32[]{:S(2)}, u32[]{:S(2)}) collective-permute-start(bf16[192,1536]{1,0:T(8,128)(2,1)S(1)} %get-tuple-element.145), channel_id=1, source_target_pairs={{32,0},{48,16},{64,32},{80,48},{96,64},{112,80},{0,96},{16,112},{3... | collective-permute-start | bytes 1769480 | tf_op jit(solution)/shard_map/ppermute | solution.py:49
  106.9 12.1 %collective-permute-start.14 = (bf16[192,1024]{1,0:T(8,128)(2,1)S(1)}, bf16[192,1024]{1,0:T(8,128)(2,1)S(1)}, u32[]{:S(2)}, u32[]{:S(2)}) collective-permute-start(bf16[192,1024]{1,0:T(8,128)(2,1)S(1)} %get-tuple-element.141), channel_id=1, source_target_pairs={{96,0},{112,16},{0,32},{16,48},{32,64},{48,80},{64,96},{80,112},{9... | collective-permute-start | bytes 1179656 | tf_op jit(solution)/shard_map/ppermute | solution.py:49
  108.4 17.9 %collective-permute-start.13 = (bf16[192,1024]{1,0:T(8,128)(2,1)S(1)}, bf16[192,1024]{1,0:T(8,128)(2,1)S(1)}, u32[]{:S(2)}, u32[]{:S(2)}) collective-permute-start(bf16[192,1024]{1,0:T(8,128)(2,1)S(1)} %get-tuple-element.141), channel_id=1, source_target_pairs={{64,0},{80,16},{96,32},{112,48},{0,64},{16,80},{32,96},{48,112},{6... | collective-permute-start | bytes 1179656 | tf_op jit(solution)/shard_map/ppermute | solution.py:49
  111.1 15.2 %collective-permute-start.12 = (bf16[192,1024]{1,0:T(8,128)(2,1)S(1)}, bf16[192,1024]{1,0:T(8,128)(2,1)S(1)}, u32[]{:S(2)}, u32[]{:S(2)}) collective-permute-start(bf16[192,1024]{1,0:T(8,128)(2,1)S(1)} %get-tuple-element.141), channel_id=1, source_target_pairs={{32,0},{48,16},{64,32},{80,48},{96,64},{112,80},{0,96},{16,112},{3... | collective-permute-start | bytes 1179656 | tf_op jit(solution)/shard_map/ppermute | solution.py:49
  126.6 8.0 %collective-permute-start.19 = (bf16[4,192,1536]{2,1,0:T(8,128)(2,1)S(1)}, bf16[4,192,1536]{2,1,0:T(8,128)(2,1)}, u32[]{:S(2)}, u32[]{:S(2)}) collective-permute-start(bf16[4,192,1536]{2,1,0:T(8,128)(2,1)S(1)} %pad_maximum_fusion.out_near_ref), channel_id=1, source_target_pairs={{16,0},{0,16},{48,32},{32,48},{80,64},{64,80},{112,96},{96,112},{1... | collective-permute-start | bytes 7077896 | tf_op jit(solution)/shard_map/ppermute | solution.py:54
  128.0 5.5 %collective-permute-start.18 = (bf16[4,192,1024]{2,1,0:T(8,128)(2,1)S(1)}, bf16[4,192,1024]{2,1,0:T(8,128)(2,1)S(1)}, u32[]{:S(2)}, u32[]{:S(2)}) collective-permute-start(bf16[4,192,1024]{2,1,0:T(8,128)(2,1)S(1)} %pad_maximum_fusion.1.near_ref), channel_id=1, source_target_pairs={{16,0},{0,16},{48,32},{32,48},{80,64},{64,80},{112,96},{96,112},{1... | collective-permute-start | bytes 4718600 | tf_op jit(solution)/shard_map/ppermute | solution.py:54
  153.9 3.7 collective-permute-start.20
  160.5 13.9 %collective-permute-start.23 = (bf16[128,1536]{1,0:T(8,128)(2,1)}, bf16[128,1536]{1,0:T(8,128)(2,1)}, u32[]{:S(2)}, u32[]{:S(2)}) collective-permute-start(bf16[128,1536]{1,0:T(8,128)(2,1)} %get-tuple-element.284), channel_id=1, source_target_pairs={{0,64},{16,80},{32,96},{48,112},{64,0},{80,16},{96,32},{112,48},{1... | collective-permute-start | bytes 1179656 | tf_op jit(solution)/shard_map/ppermute | solution.py:67
  163.1 18.4 %collective-permute-start.22 = (bf16[128,1536]{1,0:T(8,128)(2,1)}, bf16[128,1536]{1,0:T(8,128)(2,1)}, u32[]{:S(2)}, u32[]{:S(2)}) collective-permute-start(bf16[128,1536]{1,0:T(8,128)(2,1)} %get-tuple-element.285), channel_id=1, source_target_pairs={{0,96},{16,112},{32,0},{48,16},{64,32},{80,48},{96,64},{112,80},{1... | collective-permute-start | bytes 1179656 | tf_op jit(solution)/shard_map/ppermute | solution.py:67
  164.5 17.4 %collective-permute-start.21 = (bf16[128,1536]{1,0:T(8,128)(2,1)}, bf16[128,1536]{1,0:T(8,128)(2,1)}, u32[]{:S(2)}, u32[]{:S(2)}) collective-permute-start(bf16[128,1536]{1,0:T(8,128)(2,1)} %get-tuple-element.286), channel_id=1, source_target_pairs={{0,32},{16,48},{32,64},{48,80},{64,96},{80,112},{96,0},{112,16},{1... | collective-permute-start | bytes 1179656 | tf_op jit(solution)/shard_map/ppermute | solution.py:67
  184.9 13.4 %collective-permute-start.26 = (bf16[128,1536]{1,0:T(8,128)(2,1)}, bf16[128,1536]{1,0:T(8,128)(2,1)S(1)}, u32[]{:S(2)}, u32[]{:S(2)}) collective-permute-start(bf16[128,1536]{1,0:T(8,128)(2,1)} %get-tuple-element.157), channel_id=1, source_target_pairs={{96,0},{112,16},{0,32},{16,48},{32,64},{48,80},{64,96},{80,112},{9... | collective-permute-start | bytes 1179656 | tf_op jit(solution)/shard_map/ppermute | solution.py:49
  186.5 20.0 %collective-permute-start.25 = (bf16[128,1536]{1,0:T(8,128)(2,1)}, bf16[128,1536]{1,0:T(8,128)(2,1)S(1)}, u32[]{:S(2)}, u32[]{:S(2)}) collective-permute-start(bf16[128,1536]{1,0:T(8,128)(2,1)} %get-tuple-element.157), channel_id=1, source_target_pairs={{64,0},{80,16},{96,32},{112,48},{0,64},{16,80},{32,96},{48,112},{6... | collective-permute-start | bytes 1179656 | tf_op jit(solution)/shard_map/ppermute | solution.py:49
  188.9 17.8 %collective-permute-start.24 = (bf16[128,1536]{1,0:T(8,128)(2,1)}, bf16[128,1536]{1,0:T(8,128)(2,1)S(1)}, u32[]{:S(2)}, u32[]{:S(2)}) collective-permute-start(bf16[128,1536]{1,0:T(8,128)(2,1)} %get-tuple-element.157), channel_id=1, source_target_pairs={{32,0},{48,16},{64,32},{80,48},{96,64},{112,80},{0,96},{16,112},{3... | collective-permute-start | bytes 1179656 | tf_op jit(solution)/shard_map/ppermute | solution.py:49
  239.9 19.6 %collective-permute-start.31 = (bf16[192,1024]{1,0:T(8,128)(2,1)S(1)}, bf16[192,1024]{1,0:T(8,128)(2,1)S(1)}, u32[]{:S(2)}, u32[]{:S(2)}) collective-permute-start(bf16[192,1024]{1,0:T(8,128)(2,1)S(1)} %get-tuple-element.280), channel_id=1, source_target_pairs={{0,64},{16,80},{32,96},{48,112},{64,0},{80,16},{96,32},{112,48},{1... | collective-permute-start | bytes 1179656 | tf_op jit(solution)/shard_map/ppermute | solution.py:67
  242.6 18.5 %collective-permute-start.30 = (bf16[192,1024]{1,0:T(8,128)(2,1)S(1)}, bf16[192,1024]{1,0:T(8,128)(2,1)S(1)}, u32[]{:S(2)}, u32[]{:S(2)}) collective-permute-start(bf16[192,1024]{1,0:T(8,128)(2,1)S(1)} %get-tuple-element.281), channel_id=1, source_target_pairs={{0,96},{16,112},{32,0},{48,16},{64,32},{80,48},{96,64},{112,80},{1... | collective-permute-start | bytes 1179656 | tf_op jit(solution)/shard_map/ppermute | solution.py:67
  244.4 16.7 %collective-permute-start.29 = (bf16[192,1024]{1,0:T(8,128)(2,1)S(1)}, bf16[192,1024]{1,0:T(8,128)(2,1)S(1)}, u32[]{:S(2)}, u32[]{:S(2)}) collective-permute-start(bf16[192,1024]{1,0:T(8,128)(2,1)S(1)} %get-tuple-element.282), channel_id=1, source_target_pairs={{0,32},{16,48},{32,64},{48,80},{64,96},{80,112},{96,0},{112,16},{1... | collective-permute-start | bytes 1179656 | tf_op jit(solution)/shard_map/ppermute | solution.py:67
  261.1 4.5 %collective-permute-start.32 = (bf16[4,192,1536]{2,1,0:T(8,128)(2,1)S(1)}, bf16[4,192,1536]{2,1,0:T(8,128)(2,1)S(1)}, u32[]{:S(2)}, u32[]{:S(2)}) collective-permute-start(bf16[4,192,1536]{2,1,0:T(8,128)(2,1)S(1)} %get-tuple-element.179), channel_id=1, source_target_pairs={{16,0},{0,16},{48,32},{32,48},{80,64},{64,80},{112,96},{96,112},{1... | collective-permute-start | bytes 7077896 | tf_op jit(solution)/shard_map/ppermute | solution.py:62
  266.3 17.1 %collective-permute-start.33 = (bf16[192,1536]{1,0:T(8,128)(2,1)S(1)}, bf16[192,1536]{1,0:T(8,128)(2,1)S(1)}, u32[]{:S(2)}, u32[]{:S(2)}) collective-permute-start(bf16[192,1536]{1,0:T(8,128)(2,1)S(1)} %get-tuple-element.277), channel_id=1, source_target_pairs={{0,64},{16,80},{32,96},{48,112},{64,0},{80,16},{96,32},{112,48},{1... | collective-permute-start | bytes 1769480 | tf_op jit(solution)/shard_map/ppermute | solution.py:1097
  283.4 18.6 %collective-permute-start.34 = (bf16[192,1536]{1,0:T(8,128)(2,1)S(1)}, bf16[192,1536]{1,0:T(8,128)(2,1)S(1)}, u32[]{:S(2)}, u32[]{:S(2)}) collective-permute-start(bf16[192,1536]{1,0:T(8,128)(2,1)S(1)} %get-tuple-element.187), channel_id=1, source_target_pairs={{0,32},{16,48},{32,64},{48,80},{64,96},{80,112},{96,0},{112,16},{1... | collective-permute-start | bytes 1769480 | tf_op jit(solution)/shard_map/ppermute | solution.py:1107
  285.2 16.8 %collective-permute-start.35 = (bf16[192,1536]{1,0:T(8,128)(2,1)S(1)}, bf16[192,1536]{1,0:T(8,128)(2,1)}, u32[]{:S(2)}, u32[]{:S(2)}) collective-permute-start(bf16[192,1536]{1,0:T(8,128)(2,1)S(1)} %get-tuple-element.188), channel_id=1, source_target_pairs={{0,96},{16,112},{32,0},{48,16},{64,32},{80,48},{96,64},{112,80},{1... | collective-permute-start | bytes 1769480 | tf_op jit(solution)/shard_map/ppermute | solution.py:1107
  326.9 10.1 %collective-permute-start.37 = (bf16[560,128]{1,0:T(8,128)(2,1)S(1)}, bf16[560,128]{1,0:T(8,128)(2,1)S(1)}, u32[]{:S(2)}, u32[]{:S(2)}) collective-permute-start(bf16[560,128]{1,0:T(8,128)(2,1)S(1)} %get-tuple-element.288), channel_id=1, source_target_pairs={{0,32},{16,48},{32,64},{48,80},{64,96},{80,112},{96,0},{112,16},{1... | collective-permute-start | bytes 430088 | tf_op jit(solution)/shard_map/ppermute | solution.py:67
  327.3 9.8 %collective-permute-start.39 = (bf16[560,128]{1,0:T(8,128)(2,1)S(1)}, bf16[560,128]{1,0:T(8,128)(2,1)S(1)}, u32[]{:S(2)}, u32[]{:S(2)}) collective-permute-start(bf16[560,128]{1,0:T(8,128)(2,1)S(1)} %get-tuple-element.289), channel_id=1, source_target_pairs={{0,64},{16,80},{32,96},{48,112},{64,0},{80,16},{96,32},{112,48},{1... | collective-permute-start | bytes 430088 | tf_op jit(solution)/shard_map/ppermute | solution.py:67
  329.6 8.1 %collective-permute-start.38 = (bf16[560,128]{1,0:T(8,128)(2,1)S(1)}, bf16[560,128]{1,0:T(8,128)(2,1)S(1)}, u32[]{:S(2)}, u32[]{:S(2)}) collective-permute-start(bf16[560,128]{1,0:T(8,128)(2,1)S(1)} %get-tuple-element.290), channel_id=1, source_target_pairs={{0,96},{16,112},{32,0},{48,16},{64,32},{80,48},{96,64},{112,80},{1... | collective-permute-start | bytes 430088 | tf_op jit(solution)/shard_map/ppermute | solution.py:67
  330.8 23.3 %collective-permute-start.40 = (bf16[4,192,384]{2,1,0:T(8,128)(2,1)}, bf16[4,192,384]{2,1,0:T(8,128)(2,1)S(1)}, u32[]{:S(2)}, u32[]{:S(2)}) collective-permute-start(bf16[4,192,384]{2,1,0:T(8,128)(2,1)} %get-tuple-element.203), channel_id=1, source_target_pairs={{0,1},{1,2},{2,3},{3,0},{4,5},{5,6},{6,7},{7,4},{8,9},{9,10},{10,1... | collective-permute-start | bytes 1769480 | tf_op jit(solution)/shard_map/ppermute | solution.py:1115
  334.2 19.9 %collective-permute-start.41 = (bf16[4,192,384]{2,1,0:T(8,128)(2,1)}, bf16[4,192,384]{2,1,0:T(8,128)(2,1)S(1)}, u32[]{:S(2)}, u32[]{:S(2)}) collective-permute-start(bf16[4,192,384]{2,1,0:T(8,128)(2,1)} %get-tuple-element.204), channel_id=1, source_target_pairs={{0,3},{1,0},{2,1},{3,2},{4,7},{5,4},{6,5},{7,6},{8,11},{9,8},{10,9... | collective-permute-start | bytes 1769480 | tf_op jit(solution)/shard_map/ppermute | solution.py:1115
  339.8 15.1 %all-to-all-start.2 = ((bf16[16,40,128]{2,1,0:T(8,128)(2,1)}), bf16[16,40,128]{2,1,0:T(8,128)(2,1)S(1)}, u32[]{:S(2)}, u32[]{:S(2)}) async-start(bf16[16,40,128]{2,1,0:T(8,128)(2,1)} %pad_maximum_fusion.13), calls=%async_computation.2 | async-start | bytes 327680 | tf_op jit(solution)/shard_map/all_to_all | solution.py:1124
  367.5 16.2 %collective-permute-start.42 = (bf16[4,192,384]{2,1,0:T(8,128)(2,1)}, bf16[4,192,384]{2,1,0:T(8,128)(2,1)}, u32[]{:S(2)}, u32[]{:S(2)}) collective-permute-start(bf16[4,192,384]{2,1,0:T(8,128)(2,1)} %get-tuple-element.208), channel_id=1, source_target_pairs={{0,2},{1,3},{2,0},{3,1},{4,6},{5,7},{6,4},{7,5},{8,10},{9,11},{10,... | collective-permute-start | bytes 1769480 | tf_op jit(solution)/shard_map/ppermute | solution.py:1131
  370.9 20.0 %all-to-all-start.4 = ((bf16[8,16,32,128]{3,2,1,0:T(8,128)(2,1)}), bf16[8,16,32,128]{3,2,1,0:T(8,128)(2,1)S(1)}, u32[]{:S(2)}, u32[]{:S(2)}) async-start(bf16[8,16,32,128]{3,2,1,0:T(8,128)(2,1)} %broadcast_in_dim.11), calls=%async_computation.4 | async-start | bytes 2097152 | tf_op jit(solution)/shard_map/all_to_all | solution.py:96
  385.8 12.1 %collective-permute-start.45 = (bf16[192,384]{1,0:T(8,128)(2,1)}, bf16[192,384]{1,0:T(8,128)(2,1)}, u32[]{:S(2)}, u32[]{:S(2)}) collective-permute-start(bf16[192,384]{1,0:T(8,128)(2,1)} %get-tuple-element.293), channel_id=1, source_target_pairs={{0,8},{1,9},{2,10},{3,11},{4,12},{5,13},{6,14},{7,15},{8,0},{9,1},... | collective-permute-start | bytes 442376 | tf_op jit(solution)/shard_map/ppermute | solution.py:91
  387.5 10.5 %collective-permute-start.44 = (bf16[192,384]{1,0:T(8,128)(2,1)}, bf16[192,384]{1,0:T(8,128)(2,1)}, u32[]{:S(2)}, u32[]{:S(2)}) collective-permute-start(bf16[192,384]{1,0:T(8,128)(2,1)} %get-tuple-element.294), channel_id=1, source_target_pairs={{0,12},{1,13},{2,14},{3,15},{4,0},{5,1},{6,2},{7,3},{8,4},{9,5},{1... | collective-permute-start | bytes 442376 | tf_op jit(solution)/shard_map/ppermute | solution.py:91
  389.0 9.0 %collective-permute-start.43 = (bf16[192,384]{1,0:T(8,128)(2,1)S(1)}, bf16[192,384]{1,0:T(8,128)(2,1)}, u32[]{:S(2)}, u32[]{:S(2)}) collective-permute-start(bf16[192,384]{1,0:T(8,128)(2,1)S(1)} %get-tuple-element.295), channel_id=1, source_target_pairs={{0,4},{1,5},{2,6},{3,7},{4,8},{5,9},{6,10},{7,11},{8,12},{9,13},{1... | collective-permute-start | bytes 442376 | tf_op jit(solution)/shard_map/ppermute | solution.py:91
  (57 other events, 690.3 us)
Sparse Core Ops, SparseCore 0:
  67.3 55.4 all-gather.1
  283.6 89.1 reduce-scatter.1
